TPU v7x, 32 devices: a whole 2x2x4 slice. The times are simulated.
32 devices in a mesh: dp: 8 (over z, x), blk: 4 (over y, core).
Axes of the slice: x: 2, y: 2, z: 4, core: 2. Of those that a mesh axis runs over, the one named last changes fastest.
Arguments:
- tokens: bfloat16 [8, 1024, 768], P('dp', 'blk'), may hold values from -6 to 6
- segments: int32 [8, 1024], P('dp', 'blk'), may hold values from 0 to 2, as said below
- positions: int32 [8, 1024], P('dp', 'blk'), may hold values from 0 to 1008, as said below
- cotangent: bfloat16 [8, 1024, 768], P('dp', 'blk'), may hold values from -6 to 6
- attn_gain: bfloat16 [768], P(('dp', 'blk')), may hold values from 0.5 to 1.5
- w_query: bfloat16 [768, 768], P(('dp', 'blk')), may hold values from -0.3125 to 0.3125
- w_key: bfloat16 [768, 768], P(('dp', 'blk')), may hold values from -0.3125 to 0.3125
- w_value: bfloat16 [768, 768], P(('dp', 'blk')), may hold values from -0.21875 to 0.21875
- w_out: bfloat16 [768, 768], P(('dp', 'blk')), may hold values from -1.75 to 1.75
- mlp_gain: bfloat16 [768], P(('dp', 'blk')), may hold values from 0.5 to 1.5
- w_gate: bfloat16 [768, 2048], P(('dp', 'blk')), may hold values from -0.21875 to 0.21875
- w_up: bfloat16 [768, 2048], P(('dp', 'blk')), may hold values from -0.21875 to 0.21875
- w_down: bfloat16 [2048, 768], P(('dp', 'blk')), may hold values from -0.1875 to 0.1875
Outputs:
- output: bfloat16 [8, 1024, 768], P('dp', 'blk')
- grad_tokens: bfloat16 [8, 1024, 768], P('dp', 'blk')
- grad_attn_gain: float32 [768], P(('dp', 'blk'))
- grad_w_query: float32 [768, 768], P(('dp', 'blk'))
- grad_w_key: float32 [768, 768], P(('dp', 'blk'))
- grad_w_value: float32 [768, 768], P(('dp', 'blk'))
- grad_w_out: float32 [768, 768], P(('dp', 'blk'))
- grad_mlp_gain: float32 [768], P(('dp', 'blk'))
- grad_w_gate: float32 [768, 2048], P(('dp', 'blk'))
- grad_w_up: float32 [768, 2048], P(('dp', 'blk'))
- grad_w_down: float32 [2048, 768], P(('dp', 'blk'))
Inputs may be any that keep to these rules, and one draw needn't show every extreme that they name: `segments`: each pack holds three documents in order: the first, of 1 + 24 h slots, ends within the first 256 slots; the second, of 1 + 24 h slots, ends within the last 256 slots; the third fills the rest. `positions`: the index of each slot within its document, as given by segments.
All inputs are finite; a program needn't handle non-finite values.
Results may differ from a plain program's by a relative error of at most 0.03.
Values may be sent and summed in bfloat16 or wider, within the bound.
No kernel may reach another device: no remote copies, remote signals or barrier semaphores. Data moves between devices by JAX's collectives and lax.ppermute only.
A program may use at most 192 MiB of HBM per device.

v0:
```python
import math

import jax
import jax.numpy as jnp
from jax import lax
from jax.sharding import PartitionSpec as P

HEADS = 12
HEAD_DIM = 64


EPS = 1e-05
SCALE = 0.125
NEG = -1e30


def rope_tables(slot_positions, half_dim):
    inverse = jnp.exp(-math.log(10000.0) * jnp.arange(half_dim, dtype=jnp.float32) / half_dim)
    angles = slot_positions.astype(jnp.float32)[:, None] * inverse[None, :]
    return (jnp.cos(angles)[:, None, :], jnp.sin(angles)[:, None, :])


def rotate(tensor, cosine_table, sine_table):
    half_dim = tensor.shape[-1] // 2
    leading = tensor[..., :half_dim]
    trailing = tensor[..., half_dim:]
    return jnp.concatenate(
        [
            leading * cosine_table - trailing * sine_table,
            trailing * cosine_table + leading * sine_table,
        ],
        axis=-1,
    )


def matmul(left_matrix, right_matrix):
    return jnp.dot(left_matrix, right_matrix, preferred_element_type=jnp.float32)


def left_product(left_matrix, right_matrix):
    return lax.dot_general(
        left_matrix, right_matrix, (((0,), (0,)), ((), ())), preferred_element_type=jnp.float32
    )


def right_product(left_matrix, right_matrix):
    return lax.dot_general(
        left_matrix, right_matrix, (((1,), (1,)), ((), ())), preferred_element_type=jnp.float32
    )


def norm_back(grad_normed, values, inverse, gain):
    unit_normed = values * inverse
    scaled = grad_normed * gain
    grad_gain = jnp.sum(grad_normed * unit_normed, axis=0)
    grad_values = inverse * (
        scaled - unit_normed * jnp.mean(scaled * unit_normed, axis=-1, keepdims=True)
    )
    return (grad_values, grad_gain)


def score_mask(query_segments, query_index, key_segments, key_index):
    return (query_segments[:, None] == key_segments[None, :]) & (
        key_index[None, :] <= query_index[:, None]
    )


def block_grads(query_block, grad_block, lse_rows, delta_rows, allowed, key_block, value_block):
    scores = (
        jnp.einsum("qhd,khd->hqk", query_block, key_block, preferred_element_type=jnp.float32)
        * SCALE
    )
    probability = jnp.exp(jnp.where(allowed[None], scores - lse_rows.T[:, :, None], NEG))
    grad_value = jnp.einsum(
        "hqk,qhd->khd",
        probability.astype(jnp.bfloat16),
        grad_block,
        preferred_element_type=jnp.float32,
    )
    grad_probs = jnp.einsum(
        "qhd,khd->hqk", grad_block, value_block, preferred_element_type=jnp.float32
    )
    grad_scores = (probability * (grad_probs - delta_rows.T[:, :, None])).astype(jnp.bfloat16)
    grad_query = (
        jnp.einsum("hqk,khd->qhd", grad_scores, key_block, preferred_element_type=jnp.float32)
        * SCALE
    )
    grad_key = (
        jnp.einsum("hqk,qhd->khd", grad_scores, query_block, preferred_element_type=jnp.float32)
        * SCALE
    )
    return (grad_query, grad_key, grad_value)


def shards(
    tokens,
    segments,
    positions,
    cotangent,
    attn_gain,
    w_query,
    w_key,
    w_value,
    w_out,
    mlp_gain,
    w_gate,
    w_up,
    w_down,
):
    local_rows = tokens.shape[1]
    model_width = tokens.shape[2]
    blocks = lax.axis_size("blk")
    own_start = lax.axis_index("blk") * local_rows
    query_index = own_start + jnp.arange(local_rows, dtype=jnp.int32)
    own_segments = segments[0]
    cosine_table, sine_table = rope_tables(positions[0], HEAD_DIM // 2)
    x_float = tokens[0].astype(jnp.float32)
    gathered = (
        lax.all_gather(attn_gain, ("dp", "blk"), axis=0, tiled=True),
        lax.all_gather(w_query, ("dp", "blk"), axis=0, tiled=True),
        lax.all_gather(w_key, ("dp", "blk"), axis=0, tiled=True),
        lax.all_gather(w_value, ("dp", "blk"), axis=0, tiled=True),
        lax.all_gather(w_out, ("dp", "blk"), axis=0, tiled=True),
        lax.all_gather(mlp_gain, ("dp", "blk"), axis=0, tiled=True),
        lax.all_gather(w_gate, ("dp", "blk"), axis=0, tiled=True),
        lax.all_gather(w_up, ("dp", "blk"), axis=0, tiled=True),
        lax.all_gather(w_down, ("dp", "blk"), axis=0, tiled=True),
    )
    gain_one = gathered[0].astype(jnp.float32)
    gain_two = gathered[5].astype(jnp.float32)
    inverse_one = lax.rsqrt(jnp.mean(x_float * x_float, axis=-1, keepdims=True) + EPS)
    normed = (x_float * inverse_one * gain_one).astype(jnp.bfloat16)
    query_rot = rotate(
        matmul(normed, gathered[1]).reshape(local_rows, HEADS, HEAD_DIM), cosine_table, sine_table
    ).astype(jnp.bfloat16)
    key_rot = rotate(
        matmul(normed, gathered[2]).reshape(local_rows, HEADS, HEAD_DIM), cosine_table, sine_table
    ).astype(jnp.bfloat16)
    value_heads = (
        matmul(normed, gathered[3]).astype(jnp.bfloat16).reshape(local_rows, HEADS, HEAD_DIM)
    )
    key_flat = key_rot.reshape(local_rows, model_width)
    value_flat = value_heads.reshape(local_rows, model_width)
    start_state = (
        jnp.full((HEADS, local_rows), NEG, jnp.float32),
        jnp.zeros((HEADS, local_rows), jnp.float32),
        jnp.zeros((local_rows, HEADS, HEAD_DIM), jnp.float32),
    )
    key_piece = lax.all_gather(key_flat, "blk", axis=0, tiled=True)
    value_piece = lax.all_gather(value_flat, "blk", axis=0, tiled=True)
    seg_piece = lax.all_gather(own_segments, "blk", axis=0, tiled=True)
    piece_rows = key_piece.shape[0]
    needed = (jnp.int32(0) <= own_start + local_rows - 1) & (
        seg_piece[piece_rows - 1] >= own_segments[0]
    )

    def attend_sweep(current):

        def attend_visit(number, partial_value):
            running_max, running_sum, weighted = partial_value
            offset = number * local_rows
            key_block = lax.dynamic_slice_in_dim(key_piece, offset, local_rows, 0).reshape(
                local_rows, HEADS, HEAD_DIM
            )
            value_block = lax.dynamic_slice_in_dim(value_piece, offset, local_rows, 0).reshape(
                local_rows, HEADS, HEAD_DIM
            )
            seg_block = lax.dynamic_slice_in_dim(seg_piece, offset, local_rows, 0)
            key_index = offset + jnp.arange(local_rows, dtype=jnp.int32)
            allowed = score_mask(own_segments, query_index, seg_block, key_index)
            scores = (
                jnp.einsum("qhd,khd->hqk", query_rot, key_block, preferred_element_type=jnp.float32)
                * SCALE
            )
            scores = jnp.where(allowed[None], scores, NEG)
            new_max = jnp.maximum(running_max, jnp.max(scores, axis=-1))
            probability = jnp.where(allowed[None], jnp.exp(scores - new_max[:, :, None]), 0.0)
            factor = jnp.exp(running_max - new_max)
            running_sum = running_sum * factor + jnp.sum(probability, axis=-1)
            weighted = weighted * factor.T[:, :, None] + jnp.einsum(
                "hqk,khd->qhd",
                probability.astype(jnp.bfloat16),
                value_block,
                preferred_element_type=jnp.float32,
            )
            return (new_max, running_sum, weighted)

        return lax.fori_loop(0, piece_rows // local_rows, attend_visit, current)

    final_max, final_sum, final_weighted = lax.cond(
        needed, attend_sweep, lambda unchanged: unchanged, start_state
    )
    attn_heads = (final_weighted / final_sum.T[:, :, None]).astype(jnp.bfloat16)
    lse_rows = (final_max + jnp.log(final_sum)).T
    attn_flat = attn_heads.reshape(local_rows, model_width)
    resid = x_float + matmul(attn_flat, gathered[4])
    inverse_two = lax.rsqrt(jnp.mean(resid * resid, axis=-1, keepdims=True) + EPS)
    normed_two = (resid * inverse_two * gain_two).astype(jnp.bfloat16)
    gate = matmul(normed_two, gathered[6])
    up_values = matmul(normed_two, gathered[7])
    hidden = (jax.nn.silu(gate) * up_values).astype(jnp.bfloat16)
    output = (resid + matmul(hidden, gathered[8])).astype(jnp.bfloat16)
    later = (
        lax.all_gather(attn_gain, ("dp", "blk"), axis=0, tiled=True),
        lax.all_gather(w_query, ("dp", "blk"), axis=0, tiled=True),
        lax.all_gather(w_key, ("dp", "blk"), axis=0, tiled=True),
        lax.all_gather(w_value, ("dp", "blk"), axis=0, tiled=True),
        lax.all_gather(w_out, ("dp", "blk"), axis=0, tiled=True),
        lax.all_gather(mlp_gain, ("dp", "blk"), axis=0, tiled=True),
        lax.all_gather(w_gate, ("dp", "blk"), axis=0, tiled=True),
        lax.all_gather(w_up, ("dp", "blk"), axis=0, tiled=True),
        lax.all_gather(w_down, ("dp", "blk"), axis=0, tiled=True),
    )
    grad_res = cotangent[0].astype(jnp.float32)
    grad_mlp = grad_res.astype(jnp.bfloat16)
    grad_down = left_product(hidden, grad_mlp)
    grad_hidden = right_product(grad_mlp, later[8])
    sigmoid_gate = jax.nn.sigmoid(gate)
    grad_gate_low = (
        grad_hidden * up_values * sigmoid_gate * (1.0 + gate * (1.0 - sigmoid_gate))
    ).astype(jnp.bfloat16)
    grad_up_low = (grad_hidden * gate * sigmoid_gate).astype(jnp.bfloat16)
    grad_gate_w = left_product(normed_two, grad_gate_low)
    grad_up_w = left_product(normed_two, grad_up_low)
    grad_normed_two = right_product(grad_gate_low, later[6]) + right_product(grad_up_low, later[7])
    grad_resid_norm, grad_gain_two = norm_back(grad_normed_two, resid, inverse_two, gain_two)
    grad_mid = grad_res + grad_resid_norm
    grad_branch = grad_mid.astype(jnp.bfloat16)
    grad_out_w = left_product(attn_flat, grad_branch)
    grad_attn = (
        right_product(grad_branch, later[4])
        .astype(jnp.bfloat16)
        .reshape(local_rows, HEADS, HEAD_DIM)
    )
    delta_rows = jnp.sum(grad_attn.astype(jnp.float32) * attn_heads.astype(jnp.float32), axis=-1)
    pack_length = local_rows * blocks
    empty_back = (
        jnp.zeros((local_rows, HEADS, HEAD_DIM), jnp.float32),
        jnp.zeros((pack_length, 2 * model_width), jnp.float32),
    )
    back_key_piece = lax.all_gather(key_flat, "blk", axis=0, tiled=True)
    back_value_piece = lax.all_gather(value_flat, "blk", axis=0, tiled=True)
    back_seg_piece = lax.all_gather(own_segments, "blk", axis=0, tiled=True)
    back_piece_rows = back_key_piece.shape[0]
    needed = (jnp.int32(0) <= own_start + local_rows - 1) & (
        back_seg_piece[back_piece_rows - 1] >= own_segments[0]
    )

    def back_sweep(current):

        def back_visit(number, partial_value):
            grad_query_acc, grad_pairs = partial_value
            offset = number * local_rows
            key_block = lax.dynamic_slice_in_dim(back_key_piece, offset, local_rows, 0).reshape(
                local_rows, HEADS, HEAD_DIM
            )
            value_block = lax.dynamic_slice_in_dim(back_value_piece, offset, local_rows, 0).reshape(
                local_rows, HEADS, HEAD_DIM
            )
            seg_block = lax.dynamic_slice_in_dim(back_seg_piece, offset, local_rows, 0)
            key_index = offset + jnp.arange(local_rows, dtype=jnp.int32)
            allowed = score_mask(own_segments, query_index, seg_block, key_index)
            part_query, part_key, part_value = block_grads(
                query_rot, grad_attn, lse_rows, delta_rows, allowed, key_block, value_block
            )
            new_rows = jnp.concatenate(
                [
                    part_key.reshape(local_rows, model_width),
                    part_value.reshape(local_rows, model_width),
                ],
                axis=1,
            )
            existing = lax.dynamic_slice_in_dim(grad_pairs, offset, local_rows, 0)
            grad_pairs = lax.dynamic_update_slice_in_dim(grad_pairs, existing + new_rows, offset, 0)
            return (grad_query_acc + part_query, grad_pairs)

        return lax.fori_loop(0, back_piece_rows // local_rows, back_visit, current)

    grad_query_rot, grad_pairs_all = lax.cond(
        needed, back_sweep, lambda unchanged: unchanged, empty_back
    )
    own_pairs = lax.psum_scatter(
        grad_pairs_all.astype(jnp.bfloat16), "blk", scatter_dimension=0, tiled=True
    ).astype(jnp.float32)
    grad_key_rot = own_pairs[:, :model_width].reshape(local_rows, HEADS, HEAD_DIM)
    grad_value_heads = own_pairs[:, model_width:].reshape(local_rows, HEADS, HEAD_DIM)
    grad_query_low = (
        rotate(grad_query_rot, cosine_table, -sine_table)
        .reshape(local_rows, model_width)
        .astype(jnp.bfloat16)
    )
    grad_key_low = (
        rotate(grad_key_rot, cosine_table, -sine_table)
        .reshape(local_rows, model_width)
        .astype(jnp.bfloat16)
    )
    grad_value_low = grad_value_heads.reshape(local_rows, model_width).astype(jnp.bfloat16)
    grad_query_w = left_product(normed, grad_query_low)
    grad_key_w = left_product(normed, grad_key_low)
    grad_value_w = left_product(normed, grad_value_low)
    grad_normed = (
        right_product(grad_query_low, later[1])
        + right_product(grad_key_low, later[2])
        + right_product(grad_value_low, later[3])
    )
    grad_x_norm, grad_gain_one = norm_back(grad_normed, x_float, inverse_one, gain_one)
    grad_input = (grad_mid + grad_x_norm).astype(jnp.bfloat16)
    summed = (
        lax.psum_scatter(grad_gain_one, ("dp", "blk"), scatter_dimension=0, tiled=True),
        lax.psum_scatter(grad_query_w, ("dp", "blk"), scatter_dimension=0, tiled=True),
        lax.psum_scatter(grad_key_w, ("dp", "blk"), scatter_dimension=0, tiled=True),
        lax.psum_scatter(grad_value_w, ("dp", "blk"), scatter_dimension=0, tiled=True),
        lax.psum_scatter(grad_out_w, ("dp", "blk"), scatter_dimension=0, tiled=True),
        lax.psum_scatter(grad_gain_two, ("dp", "blk"), scatter_dimension=0, tiled=True),
        lax.psum_scatter(grad_gate_w, ("dp", "blk"), scatter_dimension=0, tiled=True),
        lax.psum_scatter(grad_up_w, ("dp", "blk"), scatter_dimension=0, tiled=True),
        lax.psum_scatter(grad_down, ("dp", "blk"), scatter_dimension=0, tiled=True),
    )
    return (
        output.reshape(1, local_rows, model_width),
        grad_input.reshape(1, local_rows, model_width),
        summed[0],
        summed[1],
        summed[2],
        summed[3],
        summed[4],
        summed[5],
        summed[6],
        summed[7],
        summed[8],
    )


def solution(mesh):
    return jax.shard_map(
        shards,
        mesh=mesh,
        in_specs=(
            P("dp", "blk", None),
            P("dp", "blk"),
            P("dp", "blk"),
            P("dp", "blk", None),
            P(("dp", "blk")),
            P(("dp", "blk"), None),
            P(("dp", "blk"), None),
            P(("dp", "blk"), None),
            P(("dp", "blk"), None),
            P(("dp", "blk")),
            P(("dp", "blk"), None),
            P(("dp", "blk"), None),
            P(("dp", "blk"), None),
        ),
        out_specs=(
            P("dp", "blk", None),
            P("dp", "blk", None),
            P(("dp", "blk")),
            P(("dp", "blk"), None),
            P(("dp", "blk"), None),
            P(("dp", "blk"), None),
            P(("dp", "blk"), None),
            P(("dp", "blk")),
            P(("dp", "blk"), None),
            P(("dp", "blk"), None),
            P(("dp", "blk"), None),
        ),
        check_vma=False,
    )
```

profile of v0, /device:TPU:0, one launch (start us, length us, event | category | flops | bytes accessed | tf_op | source)
XLA Modules:
  0.0 1349.8 jit_solution(9965746662190681791)
XLA Ops:
  11.2 42.1 %all-reduce.5 = (bf16[768]{0:T(1024)(128)(2,1)S(1)}, bf16[768]{0:T(1024)(128)(2,1)S(1)}) all-reduce(bf16[768]{0:T(1024)(128)(2,1)S(1)} %dynamic-update-slice, bf16[768]{0:T(1024)(128)(2,1)S(1)} %dynamic-update-slice.1), channel_id=1, replica_groups=mesh['dp'=8,'blk'=4] {'dp','blk'}, use_global_device_ids=true, to_apply=%add | all-reduce | flops 1536 | bytes 6144
  54.4 13.3 all-gather.17.cloned.1.call-done
  67.7 2.7 convolution_convert_fusion.1
  71.3 52.4 %all-gather.11.cloned.1.call-done = bf16[768,768]{1,0:T(8,128)(2,1)} async-done(((bf16[24,768]{1,0:T(8,128)(2,1)}), bf16[768,768]{1,0:T(8,128)(2,1)}) %all-gather.11.cloned.1.call-update) | async-done | bytes 1179664 | tf_op jit(solution)/shard_map/all_gather | solution.py:121
  125.3 54.4 %all-gather.15.cloned.1.call-done = bf16[768,768]{1,0:T(8,128)(2,1)} async-done(((bf16[24,768]{1,0:T(8,128)(2,1)}), bf16[768,768]{1,0:T(8,128)(2,1)}) %all-gather.15.cloned.1.call-update) | async-done | bytes 1179664 | tf_op jit(solution)/shard_map/all_gather | solution.py:120
  186.9 5.5 all-gather
  195.0 5.4 all-gather.19.cloned.1.call-done
  200.3 21.8 %all-gather.13.cloned.1.call-done = bf16[1024,768]{0,1:T(8,128)(2,1)} async-done(((bf16[256,768]{0,1:T(8,128)(2,1)}), bf16[1024,768]{0,1:T(8,128)(2,1)}) %all-gather.13.cloned.1.call-update) | async-done | bytes 1572880 | tf_op jit(solution)/shard_map/all_gather | solution.py:149
  222.2 39.3 %conditional.2 = (f32[12,256]{1,0:T(8,128)}, f32[12,256]{1,0:T(8,128)}, f32[256,12,64]{0,2,1:T(8,128)}, f32[12,256]{1,0:T(8,128)S(1)}) conditional(s32[]{:T(128)} %convert_element_type.146, () %tuple.65, (s32[1,256]{1,0:T(1,128)S(1)}, s32[1024]{0:T(1024)}, s32[256]{0:T(256)S(1)}, bf16[1024,768]{0,1:T(8,128)(2,1)}, bf16[256,12,64]{0,2,1:T(8,128)(2,1)S(1)}, ...), branch_computations={%region_1.0_spmd, %region_2.7_spmd} | conditional | flops 212355328 | bytes 15039855 | solution.py:190
  222.2 38.5 %while.37 = (s32[]{:T(128)}, f32[12,256]{1,0:T(8,128)}, f32[12,256]{1,0:T(8,128)}, f32[256,12,64]{0,2,1:T(8,128)}, s32[1,256]{1,0:T(1,128)S(1)}, /*index=5*/s32[...) while((s32[]{:T(128)}, f32[12,256]{1,0:T(8,128)}, ...), condition=%wide.region_6.6_spmd.clone, body=%wide.region_3.5_spmd.clone.sunk | while | flops 212355328 | bytes 15015127 | solution.py:188
  226.8 1.8 fusion.173
  235.2 3.0 fusion.173
  245.5 3.0 fusion.173
  255.8 3.0 fusion.173
  262.7 16.3 %all-gather.21.cloned.1.call-done = bf16[768,768]{1,0:T(8,128)(2,1)} async-done(((bf16[24,768]{1,0:T(8,128)(2,1)}), bf16[768,768]{1,0:T(8,128)(2,1)}) %all-gather.21.cloned.1.call-update) | async-done | bytes 1179664 | tf_op jit(solution)/shard_map/all_gather | solution.py:123
  279.0 1.9 multiply_reduce_fusion.3
  281.1 58.9 %all-gather.25.cloned.1.call-done = bf16[768,2048]{1,0:T(8,128)(2,1)} async-done(((bf16[24,2048]{1,0:T(8,128)(2,1)}), bf16[768,2048]{1,0:T(8,128)(2,1)}) %all-gather.25.cloned.1.call-update) | async-done | bytes 3145744 | tf_op jit(solution)/shard_map/all_gather | solution.py:126
  340.0 4.3 fusion.79
  344.2 56.5 %all-gather.23.cloned.1.call-done = bf16[768,2048]{1,0:T(8,128)(2,1)} async-done(((bf16[24,2048]{1,0:T(8,128)(2,1)}), bf16[768,2048]{1,0:T(8,128)(2,1)}) %all-gather.23.cloned.1.call-update) | async-done | bytes 3145744 | tf_op jit(solution)/shard_map/all_gather | solution.py:125
  400.7 4.2 fusion.78
  404.9 56.6 %all-gather.27.cloned.1.call-done = bf16[2048,768]{1,0:T(8,128)(2,1)} async-done(((bf16[64,768]{1,0:T(8,128)(2,1)}), bf16[2048,768]{1,0:T(8,128)(2,1)}) %all-gather.27.cloned.1.call-update) | async-done | bytes 3145744 | tf_op jit(solution)/shard_map/all_gather | solution.py:127
  461.5 5.8 multiply_convert_fusion
  470.0 1.7 multiply_reduce_fusion.1
  473.2 48.5 %conditional.3 = (f32[1024,1536]{0,1:T(8,128)}, f32[256,12,32]{0,2,1:T(8,128)}, f32[256,12,32]{0,2,1:T(8,128)S(1)}) conditional(s32[]{:T(128)} %convert_element_type.146, () %tuple.67, (f32[12,256]{1,0:T(8,128)}, f32[12,256]{1,0:T(8,128)}, bf16[256,768]{1,0:T(8,128)(2,1)S(1)}, f32[256,12,64]{0,2,1:T(8,128)S(1)}, bf16[1024,768]{0,1:T(8,128)(2,1)}, ...), branch_computations={%region_9.10_spmd, %region_10.14_spmd} | conditional | flops 513540352 | bytes 40758808 | solution.py:279
  476.2 3.4 broadcast_in_dim.130
  479.7 41.3 %while.38 = (s32[]{:T(128)}, f32[256,12,64]{0,2,1:T(8,128)S(1)}, f32[1024,1536]{0,1:T(8,128)}, bf16[1024,768]{0,1:T(8,128)(2,1)}, s32[1,256]{1,0:T(1,128)S(1)}, ...) while((s32[]{:T(128)}, f32[256,12,64]{0,2,1:T(8,128)S(1)}, ...), condition=%wide.region_13.13_spmd.clone, body=%wide.region_12.12_spmd.clone.sunk | while | flops 512950528 | bytes 29306200 | solution.py:277
  487.2 2.8 fusion.164
  497.5 2.8 fusion.164
  507.8 2.8 fusion.164
  518.1 2.9 fusion.164
  522.5 4.9 convert_element_type.169
  528.4 1.9 fusion.65
  530.5 3.7 fusion.50
  535.6 3.7 fusion.83
  540.5 3.6 fusion.82
  544.2 20.2 %reduce-scatter.9.cloned.1.call-done = bf16[256,1536]{0,1:T(8,128)(2,1)} async-done(((bf16[1024,1536]{0,1:T(8,128)(2,1)}), bf16[256,1536]{0,1:T(8,128)(2,1)}) %reduce-scatter.9.cloned.1.call-update) | async-done | bytes 786448 | tf_op jit(solution)/shard_map/reduce_scatter | solution.py:282
  564.4 3.1 fusion.62
  569.0 2.0 fusion.58
  571.1 2.0 fusion.60
  573.2 4.1 fusion.32
  579.5 39.4 %all-reduce.4 = (f32[768]{0:T(1024)S(1)}, f32[768]{0:T(1024)S(1)}) all-reduce(f32[768]{0:T(1024)S(1)} %get-tuple-element.601, f32[768]{0:T(1024)S(1)} %copy-done.35), channel_id=4, replica_groups=mesh['dp'=8,'blk'=4] {'dp','blk'}, use_global_device_ids=true, to_apply=%region_17.18.clone | all-reduce | flops 1536 | bytes 12288
  621.1 49.1 %reduce-scatter.17.cloned.1.call-done = f32[24,768]{1,0:T(8,128)} async-done(((f32[768,768]{1,0:T(8,128)}), f32[24,768]{1,0:T(8,128)}) %reduce-scatter.17.cloned.1.call-update) | async-done | bytes 73744 | tf_op jit(solution)/shard_map/reduce_scatter | solution.py:313
  670.2 119.4 %reduce-scatter.23.cloned.1.call-done = f32[64,768]{1,0:T(8,128)} async-done(((f32[2048,768]{1,0:T(8,128)}), f32[64,768]{1,0:T(8,128)}) %reduce-scatter.23.cloned.1.call-update) | async-done | bytes 196624 | tf_op jit(solution)/shard_map/reduce_scatter | solution.py:317
  789.7 120.7 %reduce-scatter.21.cloned.1.call-done = f32[24,2048]{1,0:T(8,128)} async-done(((f32[768,2048]{1,0:T(8,128)}), f32[24,2048]{1,0:T(8,128)}) %reduce-scatter.21.cloned.1.call-update) | async-done | bytes 196624 | tf_op jit(solution)/shard_map/reduce_scatter | solution.py:316
  910.4 119.7 %reduce-scatter.19.cloned.1.call-done = f32[24,2048]{1,0:T(8,128)} async-done(((f32[768,2048]{1,0:T(8,128)}), f32[24,2048]{1,0:T(8,128)}) %reduce-scatter.19.cloned.1.call-update) | async-done | bytes 196624 | tf_op jit(solution)/shard_map/reduce_scatter | solution.py:315
  1030.1 104.9 %reduce-scatter.15.cloned.1.call-done = f32[24,768]{1,0:T(8,128)} async-done(((f32[768,768]{1,0:T(8,128)}), f32[24,768]{1,0:T(8,128)}) %reduce-scatter.15.cloned.1.call-update) | async-done | bytes 73744 | tf_op jit(solution)/shard_map/reduce_scatter | solution.py:312
  1135.0 103.7 %reduce-scatter.13.cloned.1.call-done = f32[24,768]{1,0:T(8,128)} async-done(((f32[768,768]{1,0:T(8,128)}), f32[24,768]{1,0:T(8,128)}) %reduce-scatter.13.cloned.1.call-update) | async-done | bytes 73744 | tf_op jit(solution)/shard_map/reduce_scatter | solution.py:311
  1238.7 104.6 %reduce-scatter.11.cloned.1.call-done = f32[24,768]{1,0:T(8,128)} async-done(((f32[768,768]{1,0:T(8,128)}), f32[24,768]{1,0:T(8,128)}) %reduce-scatter.11.cloned.1.call-update) | async-done | bytes 73744 | tf_op jit(solution)/shard_map/reduce_scatter | solution.py:310
  (273 shorter events, 93.4 us)
Async XLA Ops:
  7.2 63.3 %copy-start.38 = (s32[1,256]{1,0:T(1,128)S(1)}, s32[1,256]{1,0:T(1,128)}, u32[]{:S(2)}) copy-start(s32[1,256]{1,0:T(1,128)} %param.23) | copy-start | bytes 3076
  7.2 60.6 %all-gather.17.cloned.1.call-start = ((), (), s32[]{:S(2)}) async-start(), calls=%async_computation.11 | async-start | bytes 1216512 | tf_op jit(solution)/shard_map/all_gather | solution.py:122
  7.9 115.8 %all-gather.11.cloned.1.call-start = ((), (), s32[]{:S(2)}) async-start(), calls=%async_computation.8 | async-start | bytes 1216512 | tf_op jit(solution)/shard_map/all_gather | solution.py:121
  8.7 171.0 %all-gather.15.cloned.1.call-start = ((), (), s32[]{:S(2)}) async-start(), calls=%async_computation.10 | async-start | bytes 1216512 | tf_op jit(solution)/shard_map/all_gather | solution.py:120
  9.4 190.9 %all-gather.19.cloned.1.call-start = ((), (), s32[]{:S(2)}) async-start(), calls=%async_computation.12 | async-start | bytes 1966080 | tf_op jit(solution)/shard_map/all_gather | solution.py:150
  54.4 127.5 %copy-start.32 = (f32[256]{0:T(256)}, f32[256]{0:T(256)S(1)}, u32[]{:S(2)}) copy-start(f32[256]{0:T(256)S(1)} %add_rsqrt_fusion.1) | copy-start | bytes 3076
  70.4 110.9 %copy-start = (bf16[1,256,768]{2,1,0:T(8,128)(2,1)S(1)}, bf16[1,256,768]{2,1,0:T(8,128)(2,1)}, u32[]{:S(2)}) copy-start(bf16[1,256,768]{2,1,0:T(8,128)(2,1)} %param.21) | copy-start | bytes 1179652
  70.4 151.7 %all-gather.13.cloned.1.call-start = ((), (), s32[]{:S(2)}) async-start(), calls=%async_computation.9 | async-start | bytes 1966080 | tf_op jit(solution)/shard_map/all_gather | solution.py:149
  71.3 111.1 %copy-start.27 = (f32[256,32]{0,1:T(8,128)}, f32[256,32]{0,1:T(8,128)S(1)}, u32[]{:S(2)}) copy-start(f32[256,32]{0,1:T(8,128)S(1)} %get-tuple-element.676) | copy-start | bytes 98308
  181.9 4.5 copy-start.30
  183.5 95.5 %all-gather.21.cloned.1.call-start = ((), (), s32[]{:S(2)}) async-start(), calls=%async_computation.13 | async-start | bytes 1216512 | tf_op jit(solution)/shard_map/all_gather | solution.py:123
  184.1 155.8 %all-gather.25.cloned.1.call-start = ((), (), s32[]{:S(2)}) async-start(), calls=%async_computation.15 | async-start | bytes 3244032 | tf_op jit(solution)/shard_map/all_gather | solution.py:126
  184.9 215.9 %all-gather.23.cloned.1.call-start = ((), (), s32[]{:S(2)}) async-start(), calls=%async_computation.14 | async-start | bytes 3244032 | tf_op jit(solution)/shard_map/all_gather | solution.py:125
  185.6 275.9 %all-gather.27.cloned.1.call-start = ((), (), s32[]{:S(2)}) async-start(), calls=%async_computation.16 | async-start | bytes 3244032 | tf_op jit(solution)/shard_map/all_gather | solution.py:127
  186.3 378.1 %reduce-scatter.9.cloned.1.call-start = ((), (), s32[]{:S(2)}) async-start(), calls=%async_computation.17 | async-start | bytes 3932160 | tf_op jit(solution)/shard_map/reduce_scatter | solution.py:282
  261.4 82.8 %copy-start.31 = (f32[12,256]{1,0:T(8,128)}, f32[12,256]{1,0:T(8,128)S(1)}, u32[]{:S(2)}) copy-start(f32[12,256]{1,0:T(8,128)S(1)} %get-tuple-element.491) | copy-start | bytes 36868
  262.7 18.2 %copy-start.9 = (bf16[256,12,64]{0,2,1:T(8,128)(2,1)}, bf16[256,12,64]{0,2,1:T(8,128)(2,1)S(1)}, u32[]{:S(2)}) copy-start(bf16[256,12,64]{0,2,1:T(8,128)(2,1)S(1)} %get-tuple-element.654) | copy-start | bytes 1179652
  280.9 190.9 %copy-start.2 = (f32[256,768]{1,0:T(8,128)}, f32[256,768]{1,0:T(8,128)S(1)}, u32[]{:S(2)}) copy-start(f32[256,768]{1,0:T(8,128)S(1)} %get-tuple-element.678) | copy-start | bytes 2359300
  280.9 187.5 %copy-start.37 = (f32[256]{0:T(256)}, f32[256]{0:T(256)S(1)}, u32[]{:S(2)}) copy-start(f32[256]{0:T(256)S(1)} %add_rsqrt_fusion) | copy-start | bytes 3076
  344.2 117.3 %copy-start.17 = (bf16[1,256,768]{2,1,0:T(8,128)(2,1)S(1)}, bf16[1,256,768]{2,1,0:T(8,128)(2,1)}, u32[]{:S(2)}) copy-start(bf16[1,256,768]{2,1,0:T(8,128)(2,1)} %param.24) | copy-start | bytes 1179652
  461.5 5.8 copy-start.13
  467.4 4.4 copy-start.7
  467.4 4.4 copy-start.25
  467.4 2.6 copy-start.1
  470.0 2.7 copy-start.5
  503.0 1.8 copy-start.16
  503.0 1.8 copy-start.23
  513.3 1.8 copy-start.16
  513.4 1.7 copy-start.23
  527.5 3.0 copy-start.14
  527.5 3.0 copy-start.19
  527.5 142.7 %reduce-scatter.17.cloned.1.call-start = ((), (), s32[]{:S(2)}) async-start(), calls=%async_computation.21 | async-start | bytes 2433024 | tf_op jit(solution)/shard_map/reduce_scatter | solution.py:313
  530.4 259.3 %reduce-scatter.23.cloned.1.call-start = ((), (), s32[]{:S(2)}) async-start(), calls=%async_computation.24 | async-start | bytes 6488064 | tf_op jit(solution)/shard_map/reduce_scatter | solution.py:317
  534.2 376.2 %reduce-scatter.21.cloned.1.call-start = ((), (), s32[]{:S(2)}) async-start(), calls=%async_computation.23 | async-start | bytes 6488064 | tf_op jit(solution)/shard_map/reduce_scatter | solution.py:316
  539.3 490.8 %reduce-scatter.19.cloned.1.call-start = ((), (), s32[]{:S(2)}) async-start(), calls=%async_computation.22 | async-start | bytes 6488064 | tf_op jit(solution)/shard_map/reduce_scatter | solution.py:315
  544.1 20.3 %copy-start.33 = (f32[256]{0:T(256)S(1)}, f32[256]{0:T(256)}, u32[]{:S(2)}) copy-start(f32[256]{0:T(256)} %copy-done.32) | copy-start | bytes 3076
  544.2 23.5 %copy-start.21 = (f32[256,12,32]{0,2,1:T(8,128)S(1)}, f32[256,12,32]{0,2,1:T(8,128)}, u32[]{:S(2)}) copy-start(f32[256,12,32]{0,2,1:T(8,128)} %copy-done.20) | copy-start | bytes 1179652
  544.2 23.5 %copy-start.28 = (f32[256,32]{0,1:T(8,128)S(1)}, f32[256,32]{0,1:T(8,128)}, u32[]{:S(2)}) copy-start(f32[256,32]{0,1:T(8,128)} %copy-done.27) | copy-start | bytes 98308
  544.2 23.5 %copy-start.29 = (f32[256,32]{0,1:T(8,128)S(1)}, f32[256,32]{0,1:T(8,128)}, u32[]{:S(2)}) copy-start(f32[256,32]{0,1:T(8,128)} %get-tuple-element.674) | copy-start | bytes 98308
  544.2 590.8 %reduce-scatter.15.cloned.1.call-start = ((), (), s32[]{:S(2)}) async-start(), calls=%async_computation.20 | async-start | bytes 2433024 | tf_op jit(solution)/shard_map/reduce_scatter | solution.py:312
  564.4 3.2 slice-start
  567.5 671.1 %reduce-scatter.13.cloned.1.call-start = ((), (), s32[]{:S(2)}) async-start(), calls=%async_computation.19 | async-start | bytes 2433024 | tf_op jit(solution)/shard_map/reduce_scatter | solution.py:311
  569.0 4.1 copy-start.11
  571.0 2.1 copy-start.3
  571.1 772.2 %reduce-scatter.11.cloned.1.call-start = ((), (), s32[]{:S(2)}) async-start(), calls=%async_computation.18 | async-start | bytes 2433024 | tf_op jit(solution)/shard_map/reduce_scatter | solution.py:310
  573.2 4.1 copy-start.6
  573.2 4.1 copy-start.12
  573.2 4.6 copy-start.4
  (21 other events, 28.6 us)
Sparse Core Ops, SparseCore 0:
  10.9 56.7 all-gather.16
  70.7 53.0 all-gather.10
  126.6 53.0 all-gather.14
  181.7 18.6 all-gather.18
  202.3 19.8 all-gather.12
  224.9 54.0 all-gather.20
  281.9 57.9 all-gather.24
  342.8 57.8 all-gather.22
  403.6 57.8 all-gather.26
  527.6 36.7 reduce-scatter.8
  571.1 99.0 reduce-scatter.16
  676.3 113.3 reduce-scatter.22
  796.8 113.5 reduce-scatter.20
  916.4 113.5 reduce-scatter.18
  1036.6 98.2 reduce-scatter.14
  1140.7 97.9 reduce-scatter.12
  1245.2 97.9 reduce-scatter.10
where the time goes:
time: 1350 us
  waiting for transfers between devices  1080 us (80%)
  blocking collectives  87 us (6%)
  matrix products  76.9 us (6%)
  local copies, waits for them, and re-layouts  46.3 us (3%)
  other arithmetic  39.7 us (3%)
  between operations  15.8 us (1%)
    reduce_scatter x1, waiting for transfers between devices, shards(): lax.psum_scatter(grad_up_w, ('dp', 'blk'), scatter_dimension=0, tiled=True)  121 us
    reduce_scatter x1, waiting for transfers between devices, shards(): lax.psum_scatter(grad_gate_w, ('dp', 'blk'), scatter_dimension=0, tiled=T...  120 us
    reduce_scatter x1, waiting for transfers between devices, shards(): lax.psum_scatter(grad_down, ('dp', 'blk'), scatter_dimension=0, tiled=True)  119 us
    reduce_scatter x1, waiting for transfers between devices, shards(): lax.psum_scatter(grad_value_w, ('dp', 'blk'), scatter_dimension=0, tiled=...  105 us
    reduce_scatter x1, waiting for transfers between devices, shards(): lax.psum_scatter(grad_query_w, ('dp', 'blk'), scatter_dimension=0, tiled=...  105 us
    reduce_scatter x1, waiting for transfers between devices, shards(): lax.psum_scatter(grad_key_w, ('dp', 'blk'), scatter_dimension=0, tiled=True)  104 us
    unnamed x2, blocking collectives  81.5 us
    all_gather x1, waiting for transfers between devices, shards(): lax.all_gather(w_up, ('dp', 'blk'), axis=0, tiled=True)  58.9 us
  transfers between devices with their start and end apart: 17, of which 17 were waited for; matrix products, arithmetic and copies ran while one was open for 7% of the time, Pallas kernels for 0%

commit v1 on v0

--- a/solution.py
+++ b/solution.py
@@ -3,6 +3,8 @@
 import jax
 import jax.numpy as jnp
 from jax import lax
+from jax.experimental import pallas as pl
+from jax.experimental.pallas import tpu as pltpu
 from jax.sharding import PartitionSpec as P
 
 HEADS = 12
@@ -331,9 +333,582 @@
     )
 
 
+BF = jnp.bfloat16
+F32 = jnp.float32
+VMEM = pltpu.VMEM
+LANES = 256
+
+
+def ids():
+    dp, blk = lax.axis_index("dp"), lax.axis_index("blk")
+    return dp // 2, dp % 2, blk // 2, blk % 2, blk
+
+
+def flip(bit, other):
+    total = 0
+    weight = 1
+    while weight <= 2:
+        own = (bit // weight) % 2
+        total = total + weight * ((1 - own) if (other // weight) % 2 else own)
+        weight *= 2
+    return total
+
+
+def aligned(value, multiple):
+    return pl.multiple_of(value, multiple)
+
+
+def dot(a, b, ca=1, cb=0):
+    return lax.dot_general(a, b, (((ca,), (cb,)), ((), ())), preferred_element_type=F32)
+
+
+def call(kernel, outs, ins, anys=0, scratch=(), flops=0, nbytes=0):
+    blocked = len(ins) - anys
+    return pl.pallas_call(
+        kernel,
+        out_shape=[jax.ShapeDtypeStruct(shape, dtype) for shape, dtype in outs],
+        in_specs=[pl.BlockSpec(memory_space=VMEM)] * blocked
+        + [pl.BlockSpec(memory_space=pl.ANY)] * anys,
+        out_specs=[pl.BlockSpec(memory_space=VMEM)] * len(outs),
+        scratch_shapes=list(scratch),
+        compiler_params=pltpu.CompilerParams(vmem_limit_bytes=56 * 1024 * 1024),
+        cost_estimate=pl.CostEstimate(flops=flops, bytes_accessed=nbytes, transcendentals=0),
+    )(*ins)
+
+
+def chip_rows(xy, zr, z, x, y):
+    return 4 * flip(z, zr) + 2 * flip(x, xy // 2) + flip(y, xy % 2)
+
+
+def assembly(pieces, dst, sems, rows, z, x, y, view=lambda ref, zr: ref.at[zr]):
+    copies = []
+    for xy in range(4):
+        for zr in range(4):
+            chip = chip_rows(xy, zr, z, x, y)
+            copies.append(
+                pltpu.make_async_copy(
+                    view(pieces[xy], zr),
+                    dst.at[pl.ds(aligned(chip * rows, rows), rows)],
+                    sems.at[4 * xy + zr],
+                )
+            )
+    return copies
+
+
+def half_swap(tile, lane):
+    return jnp.where(lane % 64 < 32, pltpu.roll(tile, 96, 1), pltpu.roll(tile, 32, 1))
+
+
+def attend_kernel(x0, x1, x2, x3, cos, sin, start, wa, wb,
+                  q_o, k_o, v_o, n_o, attn_o, lse_o, gains_o, w_o, sems):
+    z, x, y, c, b = ids()
+    copies = []
+    for xr, piece in enumerate((wa, wb)):
+        for zr in range(4):
+            dp = 2 * flip(z, zr) + flip(x, xr)
+            copies.append(
+                pltpu.make_async_copy(
+                    piece.at[zr], w_o.at[pl.ds(aligned(dp * 96, 96), 96)], sems.at[4 * xr + zr]
+                )
+            )
+    for copy in copies:
+        copy.start()
+    for copy in copies:
+        copy.wait()
+    last = w_o[:, 512:640].astype(F32).T
+    gains = last[64:72, :]
+    gains_o[...] = gains
+    gain = gains[0:1, :]
+    weights = w_o[...]
+    lane = lax.broadcasted_iota(jnp.int32, (256, 128), 1)
+    for k, piece in enumerate((x0, x1, x2, x3)):
+        rows = pl.ds(aligned(flip(b, k) * 256, 256), 256)
+        values = piece[...].astype(F32)
+        inverse = lax.rsqrt(jnp.mean(values * values, axis=-1, keepdims=True) + EPS)
+        normed = (values * inverse * gain).astype(BF)
+        n_o[rows, :] = normed
+        qkv = dot(normed, weights)
+        cosine, sine = cos[rows, :], sin[rows, :]
+        tiles = []
+        for t in range(3):
+            tile = qkv[:, 128 * t : 128 * t + 128]
+            tiles.append(tile * cosine + half_swap(tile, lane) * sine)
+        r1, r2 = pltpu.roll(tiles[1], 64, 1), pltpu.roll(tiles[2], 64, 1)
+        low = lane < 64
+        zero = jnp.zeros_like(r1)
+        q_o[rows, 0:128] = tiles[0].astype(BF)
+        q_o[rows, 128:256] = jnp.where(low, tiles[1], zero).astype(BF)
+        k_o[rows, 0:128] = jnp.where(low, r1, r2).astype(BF)
+        k_o[rows, 128:256] = jnp.where(low, r2, zero).astype(BF)
+        v_o[rows, 0:128] = qkv[:, 384:512].astype(BF)
+        v_o[rows, 128:256] = jnp.where(low, qkv[:, 512:640], zero).astype(BF)
+    head = lax.broadcasted_iota(jnp.int32, (256, LANES), 1) // 64
+    for i in range(4):
+        width = 256 * (i + 1)
+        query = q_o[256 * i : 256 * i + 256, :]
+        begin = start[256 * i : 256 * i + 256, :]
+        column = lax.broadcasted_iota(jnp.int32, (256, width), 1)
+        row = lax.broadcasted_iota(jnp.int32, (256, width), 0) + 256 * i
+        allowed = (column <= row) & (column >= begin)
+        total = jnp.zeros((256, LANES), F32)
+        stats = jnp.zeros((256, 128), F32)
+        for h in range(3):
+            mine = jnp.where(head == h, query, jnp.zeros_like(query))
+            scores = dot(mine, k_o[0:width, :], 1, 1) * SCALE
+            scores = jnp.where(allowed, scores, NEG)
+            top = jnp.max(scores, axis=-1, keepdims=True)
+            weight = jnp.exp(scores - top)
+            norm = jnp.sum(weight, axis=-1, keepdims=True)
+            mixed = dot(weight.astype(BF), v_o[0:width, :]) / norm
+            total = jnp.where(head == h, mixed, total)
+            stats = jnp.where(lane == h, top + jnp.log(norm), stats)
+        attn_o[flip(b, i)] = total.astype(BF)
+        lse_o[256 * i : 256 * i + 256, :] = stats
+
+
+def attend(xs, cos, sin, start, wa, wb):
+    outs = [((1024, LANES), BF)] * 3 + [
+        ((1024, 768), BF), ((4, 256, LANES), BF), ((1024, 128), F32), ((8, 768), F32), ((768, 640), BF),
+    ]
+    return call(
+        attend_kernel, outs, [*xs, cos, sin, start, wa, wb], anys=2,
+        scratch=[pltpu.SemaphoreType.DMA((8,))], flops=4_000_000_000, nbytes=8_000_000,
+    )
+
+
+def wo_copies(own, other, wo, sems, z, x, y, c):
+    copies = []
+    for which, pieces in enumerate((own, other)):
+        half = flip(c, which)
+        for xy in range(4):
+            for zr in range(4):
+                chip = chip_rows(xy, zr, z, x, y)
+                copies.append(
+                    pltpu.make_async_copy(
+                        pieces.at[xy, zr],
+                        wo.at[half, pl.ds(aligned(chip * 48, 48), 48)],
+                        sems.at[which, 4 * xy + zr],
+                    )
+                )
+    return copies
+
+
+def out_kernel(a0, a1, a2, a3, x0, gains, own, other, resid_o, n_o, stack_o, wo_o, sems):
+    z, x, y, c, b = ids()
+    copies = wo_copies(own, other, wo_o, sems, z, x, y, c)
+    for copy in copies:
+        copy.start()
+    for copy in copies:
+        copy.wait()
+    total = [jnp.zeros((256, 384), F32)] * 2
+    for k, piece in enumerate((a0, a1, a2, a3)):
+        rows = pl.ds(aligned(flip(b, k) * 192, 192), 192)
+        values = piece[...]
+        stack_o[k] = values
+        for half in range(2):
+            total[half] += dot(values[:, 0:192], wo_o[half, rows, :])
+    resid = x0[...].astype(F32) + jnp.concatenate(total, axis=1)
+    resid_o[...] = resid
+    inverse = lax.rsqrt(jnp.mean(resid * resid, axis=-1, keepdims=True) + EPS)
+    n_o[...] = (resid * inverse * gains[1:2, :]).astype(BF)
+
+
+def project(a, x0, gains, own, other):
+    outs = [((256, 768), F32), ((256, 768), BF), ((4, 256, LANES), BF), ((2, 768, 384), BF)]
+    return call(
+        out_kernel, outs, [*a, x0, gains, own, other], anys=2,
+        scratch=[pltpu.SemaphoreType.DMA((2, 16))], flops=400_000_000, nbytes=4_000_000,
+    )
+
+
+def hidden_kernel(n0, n1, ct0, ct1, *refs):
+    (g, u, d, (hid_o, dg_o, du_o, keep_o, send_o, wg_o, wu_o, wd_o), sems) = (
+        refs[0:4], refs[4:8], refs[8:12], refs[12:20], refs[20])
+    z, x, y, c, b = ids()
+    copies = assembly(g, wg_o, sems.at[0], 48, z, x, y, lambda ref, zr: ref.at[zr, :, pl.ds(0, 1024)])
+    copies += assembly(u, wu_o, sems.at[1], 48, z, x, y)
+    copies += assembly(d, wd_o, sems.at[2], 64, z, x, y)
+    for copy in copies:
+        copy.start()
+    for copy in copies:
+        copy.wait()
+    normed = jnp.concatenate([n0[...], n1[...]], axis=0)
+    cot = jnp.concatenate([ct0[...], ct1[...]], axis=0)
+    for j in range(4):
+        cols = slice(256 * j, 256 * j + 256)
+        gate = dot(normed, wg_o[:, cols])
+        up = dot(normed, wu_o[:, cols])
+        back = dot(cot, wd_o[cols, :], 1, 1)
+        sig = 1.0 / (1.0 + jnp.exp(-gate))
+        silu = gate * sig
+        hidden = (silu * up).astype(BF)
+        hid_o[:, cols] = hidden
+        dg_o[:, cols] = (back * up * sig * (1.0 + gate * (1.0 - sig))).astype(BF)
+        du_o[:, cols] = (back * silu).astype(BF)
+        grad = dot(hidden, cot, 0, 0)
+        for yp in range(2):
+            low, high = grad[64 * yp : 64 * yp + 64], grad[128 + 64 * yp : 192 + 64 * yp]
+            keep_o[flip(y, yp) % 2, flip(z, j)] = jnp.where(x == 0, low, high).astype(BF)
+            send_o[flip(y, yp) % 2, flip(z, j)] = jnp.where(x == 0, high, low).astype(BF)
+
+
+def hidden_and_back(n, ct, g, u, d):
+    outs = [((512, 1024), BF)] * 3 + [((2, 4, 64, 768), BF)] * 2 + [((768, 1024), BF)] * 2 + [((1024, 768), BF)]
+    return call(
+        hidden_kernel, outs, [*n, *ct, *g, *u, *d], anys=12,
+        scratch=[pltpu.SemaphoreType.DMA((3, 16))], flops=3_300_000_000, nbytes=12_000_000,
+    )
+
+
+def store_by_y(grad, cols, keep_o, send_o, z, x, y):
+    for zp in range(4):
+        for xp in range(2):
+            at = 48 * (4 * zp + 2 * xp)
+            low, high = grad[at : at + 48], grad[at + 48 : at + 96]
+            keep_o[flip(x, xp) % 2, flip(z, zp), :, cols] = jnp.where(y == 0, low, high).astype(BF)
+            send_o[flip(x, xp) % 2, flip(z, zp), :, cols] = jnp.where(y == 0, high, low).astype(BF)
+
+
+def gate_kernel(n0, n1, dg, du, wg, wu, keep_o, send_o, own_o, other_o):
+    z, x, y, c, b = ids()
+    normed = jnp.concatenate([n0[...].T, n1[...].T], axis=1)
+    for j in range(4):
+        cols = slice(256 * j, 256 * j + 256)
+        store_by_y(dot(normed, dg[:, cols]), cols, keep_o, send_o, z, x, y)
+    for t, out in enumerate((own_o, other_o)):
+        rows = slice(256 * t, 256 * t + 256)
+        out[...] = dot(dg[rows, :], wg[...], 1, 1) + dot(du[rows, :], wu[...], 1, 1)
+
+
+def gate_back(n, dg, du, wg, wu):
+    outs = [((2, 4, 48, 1024), BF)] * 2 + [((256, 768), F32)] * 2
+    return call(gate_kernel, outs, [*n, dg, du, wg, wu], flops=2_500_000_000, nbytes=9_000_000)
+
+
+def mid_kernel(gn_own, gn_in, resid, ct0, gains, wo, mid_o, branch_o, grad_o, gain_o):
+    z, x, y, c, b = ids()
+    grad = gn_own[...] + gn_in[...]
+    values = resid[...]
+    inverse = lax.rsqrt(jnp.mean(values * values, axis=-1, keepdims=True) + EPS)
+    unit = values * inverse
+    scaled = grad * gains[1:2, :]
+    gain_o[...] = jnp.broadcast_to(jnp.sum(grad * unit, axis=0, keepdims=True), gain_o.shape)
+    mid = ct0[...].astype(F32) + inverse * (
+        scaled - unit * jnp.mean(scaled * unit, axis=-1, keepdims=True)
+    )
+    mid_o[...] = mid
+    branch = mid.astype(BF)
+    branch_o[...] = branch
+    pad = jnp.zeros((256, LANES - 192), BF)
+    for k in range(4):
+        rows = pl.ds(aligned(flip(b, k) * 192, 192), 192)
+        part = dot(branch[:, 0:384], wo[0, rows, :], 1, 1) + dot(branch[:, 384:768], wo[1, rows, :], 1, 1)
+        grad_o[k] = jnp.concatenate([part.astype(BF), pad], axis=1)
+
+
+def mid_back(gn_own, gn_in, resid, ct0, gains, wo):
+    outs = [((256, 768), F32), ((256, 768), BF), ((4, 256, LANES), BF), ((8, 768), F32)]
+    return call(mid_kernel, outs, [gn_own, gn_in, resid, ct0, gains, wo], flops=400_000_000, nbytes=5_000_000)
+
+
+def up_out_kernel(n0, n1, du, s0, s1, br0, br1, keep_o, send_o, grad):
+    z, x, y, c, b = ids()
+    normed = jnp.concatenate([n0[...].T, n1[...].T], axis=1)
+    for j in range(4):
+        cols = slice(256 * j, 256 * j + 256)
+        store_by_y(dot(normed, du[:, cols]), cols, keep_o, send_o, z, x, y)
+    own = [br[:, 0:384] for br in (br0, br1)]
+    far = [br[:, 384:768] for br in (br0, br1)]
+    branch = [jnp.where(c == 0, a, f) for a, f in zip(own, far)]
+    for k in range(4):
+        part = dot(s0[k], branch[0], 0, 0) + dot(s1[k ^ 1], branch[1], 0, 0)
+        grad[pl.ds(aligned(flip(b, k) * 192, 192), 192), :] = part[0:192]
+    store_by_y(grad[...], slice(1024, 1408), keep_o, send_o, z, x, y)
+
+
+def up_out_back(n, du, s, br):
+    outs = [((2, 4, 48, 1408), BF)] * 2
+    return call(
+        up_out_kernel, outs, [*n, du, *s, *br], scratch=[pltpu.VMEM((768, 384), F32)],
+        flops=1_200_000_000, nbytes=8_000_000,
+    )
+
+
+def down_kernel(hid, wd, resid, own_o, other_o):
+    own_o[...] = resid[...] + dot(hid[0:256, :], wd[...])
+    other_o[...] = dot(hid[256:512, :], wd[...])
+
+
+def down(hid, wd, resid):
+    outs = [((256, 768), F32)] * 2
+    return call(down_kernel, outs, [hid, wd, resid], flops=800_000_000, nbytes=5_000_000)
+
+
+def attend_back_kernel(q, k, v, n, attn, g0, g1, g2, g3, lse, cos, sin, start, w, x0, x1, x2, x3, gain2,
+                       keep_o, send_o, gk_o, gs_o, do, dq, dk, dv, grads, wide):
+    z, x, y, c, b = ids()
+    for kk, piece in enumerate((g0, g1, g2, g3)):
+        do[pl.ds(aligned(flip(b, kk) * 256, 256), 256), :] = piece[...]
+    dk[...] = jnp.zeros_like(dk)
+    dv[...] = jnp.zeros_like(dv)
+    head = lax.broadcasted_iota(jnp.int32, (256, LANES), 1) // 64
+    for i in range(4):
+        width = 256 * (i + 1)
+        rows = slice(256 * i, 256 * i + 256)
+        query, out_grad = q[rows, :], do[rows, :]
+        begin = start[rows, :]
+        column = lax.broadcasted_iota(jnp.int32, (256, width), 1)
+        row = lax.broadcasted_iota(jnp.int32, (256, width), 0) + 256 * i
+        allowed = (column <= row) & (column >= begin)
+        product = out_grad.astype(F32) * attn[flip(b, i)].astype(F32)
+        total = jnp.zeros((256, LANES), F32)
+        for h in range(3):
+            here = head == h
+            mine = jnp.where(here, query, jnp.zeros_like(query))
+            ours = jnp.where(here, out_grad, jnp.zeros_like(out_grad))
+            delta = jnp.sum(jnp.where(here, product, 0.0), axis=-1, keepdims=True)
+            scores = dot(mine, k[0:width, :], 1, 1) * SCALE
+            prob = jnp.exp(jnp.where(allowed, scores - lse[rows, h : h + 1], NEG))
+            dv[0:width, :] += dot(prob.astype(BF), ours, 0, 0)
+            dprob = dot(ours, v[0:width, :], 1, 1)
+            dscore = (prob * (dprob - delta)).astype(BF)
+            dk[0:width, :] += dot(dscore, mine, 0, 0)
+            total = jnp.where(here, dot(dscore, k[0:width, :]), total)
+        dq[rows, :] = total
+    lane = lax.broadcasted_iota(jnp.int32, (256, 128), 1)
+    low = lane < 64
+    zero = jnp.zeros((256, 128), F32)
+    for i in range(4):
+        rows = slice(256 * i, 256 * i + 256)
+        cosine, sine = cos[rows, :] * SCALE, sin[rows, :] * SCALE
+        turned = []
+        for ref in (dq, dk):
+            for t in range(2):
+                tile = ref[rows, 128 * t : 128 * t + 128]
+                turned.append(tile * cosine - half_swap(tile, lane) * sine)
+        k0, k1 = pltpu.roll(turned[2], 64, 1), pltpu.roll(turned[3], 64, 1)
+        grads[rows, 0:128] = turned[0].astype(BF)
+        grads[rows, 128:256] = jnp.where(low, turned[1], k0).astype(BF)
+        grads[rows, 256:384] = jnp.where(low, k0, k1).astype(BF)
+        grads[rows, 384:512] = dv[rows, 0:128].astype(BF)
+        grads[rows, 512:640] = jnp.where(low, dv[rows, 128:256], zero).astype(BF)
+    gain_sum = jnp.zeros((1, 768), F32)
+    for kk, piece in enumerate((x0, x1, x2, x3)):
+        rows = pl.ds(aligned(flip(b, kk) * 256, 256), 256)
+        grad = dot(grads[rows, :], w[...], 1, 1)
+        values = piece[...].astype(F32)
+        inverse = lax.rsqrt(jnp.mean(values * values, axis=-1, keepdims=True) + EPS)
+        gain_sum += jnp.sum(grad * (values * inverse), axis=0, keepdims=True)
+        (gs_o if kk % 2 else gk_o)[kk // 2] = grad.astype(BF)
+    row_at = lax.broadcasted_iota(jnp.int32, (128, 768), 0)
+    gain_rows = jnp.where(row_at == 64, gain_sum, jnp.where(row_at == 65, gain2[0:1, :], 0.0))
+    gain_columns = gain_rows.T
+    normed = n[...].T
+    for j in range(5):
+        cols = slice(128 * j, 128 * j + 128)
+        part = dot(normed, grads[:, cols])
+        if j == 4:
+            part = part + gain_columns
+        wide[:, cols] = part
+    for xr, out in enumerate((keep_o, send_o)):
+        for zr in range(4):
+            dp = 2 * flip(z, zr) + flip(x, xr)
+            out[zr] = wide[pl.ds(aligned(dp * 96, 96), 96), :].astype(BF)
+
+
+def attend_back(q, k, v, n, attn, g, lse, cos, sin, start, w, xs, gain2):
+    outs = [((4, 96, 640), BF)] * 2 + [((2, 256, 768), BF)] * 2
+    return call(
+        attend_back_kernel, outs, [q, k, v, n, attn, *g, lse, cos, sin, start, w, *xs, gain2],
+        scratch=[
+            pltpu.VMEM((1024, LANES), BF), pltpu.VMEM((1024, LANES), F32), pltpu.VMEM((1024, LANES), F32),
+            pltpu.VMEM((1024, LANES), F32), pltpu.VMEM((1024, 640), BF), pltpu.VMEM((768, 640), F32),
+        ],
+        flops=10_000_000_000, nbytes=12_000_000,
+    )
+
+
+def last_kernel(kept, arrived, mid, x0, gains, out):
+    grad = kept[...].astype(F32) + arrived[...].astype(F32)
+    values = x0[...].astype(F32)
+    inverse = lax.rsqrt(jnp.mean(values * values, axis=-1, keepdims=True) + EPS)
+    unit = values * inverse
+    scaled = grad * gains[0:1, :]
+    out[...] = (
+        mid[...] + inverse * (scaled - unit * jnp.mean(scaled * unit, axis=-1, keepdims=True))
+    ).astype(BF)
+
+
+def swap_z(v, k):
+    return lax.ppermute(v, "dp", [(i, i ^ (2 * k)) for i in range(8)])
+
+
+def swap_x(v):
+    return lax.ppermute(v, "dp", [(i, i ^ 1) for i in range(8)])
+
+
+def swap_b(v, k):
+    return lax.ppermute(v, "blk", [(i, i ^ k) for i in range(4)])
+
+
+def swap_core(v):
+    return swap_b(v, 1)
+
+
+def swap_y(v):
+    return swap_b(v, 2)
+
+
+def stack_z(v):
+    return jnp.stack([v] + [swap_z(v, k) for k in (1, 2, 3)])
+
+
+def by_index(four, bits):
+    one, two = bits % 2 == 1, bits // 2 == 1
+    a, b, c, d = four
+    a, b, c, d = jnp.where(one, b, a), jnp.where(one, a, b), jnp.where(one, d, c), jnp.where(one, c, d)
+    return [jnp.where(two, c, a), jnp.where(two, d, b), jnp.where(two, a, c), jnp.where(two, b, d)]
+
+
+def sum_z(v):
+    terms = [v[0]] + [swap_z(v[k], k) for k in (1, 2, 3)]
+    return sum(term.astype(F32) for term in terms)
+
+
+def added(kept, arrived):
+    return (kept.astype(F32) + arrived.astype(F32)).astype(BF)
+
+
+def fast_shards(tokens, segments, positions, cotangent, attn_gain, w_query, w_key, w_value, w_out,
+                mlp_gain, w_gate, w_up, w_down):
+    z, x, y, c, b = ids()
+    first = c == 0
+    x0 = tokens[0]
+    ct0 = cotangent[0]
+
+    gains24 = jnp.stack([attn_gain, mlp_gain], axis=1)
+    parts = jnp.concatenate(
+        [w.reshape(24, 4, 192) for w in (w_query, w_key, w_value)]
+        + [jnp.broadcast_to(jnp.pad(gains24, ((0, 0), (0, 62)))[:, None, :], (24, 4, 64))], axis=2)
+    relative = jnp.stack(by_index([parts[:, j] for j in range(4)], b))
+    qkv_z = [relative] + [swap_z(relative, k) for k in (1, 2, 3)]
+
+    x2 = swap_y(x0)
+    x1 = swap_core(x0)
+    x3 = swap_core(x2)
+    ct1 = swap_core(ct0)
+    where_at = lax.all_gather(positions[0], "blk", axis=0, tiled=True)
+
+    gate_parts = w_gate.reshape(24, 16, 2, 64)
+    up_parts = w_up.reshape(24, 16, 2, 64)
+    out_parts = w_out.reshape(24, 2, 384)
+
+    def half(which):
+        pick = lambda a, low, high: jnp.where(first == (which == 0), low, high)
+        return jnp.concatenate(
+            [
+                pick(0, gate_parts[:, :, 0], gate_parts[:, :, 1]).reshape(24, 1024),
+                pick(0, out_parts[:, 0], out_parts[:, 1]),
+                pick(0, up_parts[:, :, 0], up_parts[:, :, 1]).reshape(24, 1024),
+            ], axis=1)
+
+    mine, theirs = half(0), half(1)
+    arrived = swap_core(theirs)
+    chip = jnp.concatenate([jnp.where(first, mine, arrived), jnp.where(first, arrived, mine)], axis=0)
+
+    to_blk = [jnp.stack([part[k] for part in qkv_z]) for k in range(4)]
+    from_blk = [to_blk[0]] + [swap_b(to_blk[k], k) for k in (1, 2, 3)]
+    qkv_a = jnp.stack(by_index(from_blk, b), axis=1).reshape(4, 96, 640)
+    qkv_b = swap_x(qkv_a)
+
+    g_z = stack_z(chip[:, :1408])
+    u_z = stack_z(chip[:, 1408:])
+    d_z = stack_z(w_down)
+    g_x, g_y = swap_x(g_z), swap_y(g_z)
+    u_y, u_x = swap_y(u_z), swap_x(u_z)
+    d_y, d_x = swap_y(d_z), swap_x(d_z)
+    g = (g_z, g_y, g_x, swap_y(g_x))
+    u = (u_z, u_y, u_x, swap_x(u_y))
+    d = (d_z, d_y, d_x, swap_x(d_y))
+    out_own = jnp.stack([piece[:, :, 1024:] for piece in g])
+    out_other = swap_core(out_own)
+
+    lane = jnp.arange(128)
+    inverse = jnp.exp(-math.log(10000.0) * (lane % 32).astype(F32) / 32)
+    angles = where_at.astype(F32)[:, None] * inverse[None, :]
+    cos = jnp.cos(angles)
+    sin = jnp.sin(angles) * jnp.where(lane % 64 < 32, -1.0, 1.0)[None, :]
+    start = (jnp.arange(1024, dtype=jnp.int32) - where_at)[:, None]
+
+    xs = (x0, x1, x2, x3)
+    q, k, v, normed, attn, lse, gains, wqkv = attend(xs, cos, sin, start, qkv_a, qkv_b)
+    a = [attn[0]] + [swap_b(attn[j], j) for j in (2, 3, 1)]
+    a = [a[0], a[3], a[1], a[2]]
+    resid, n0, s0, wo = project(a, x0, gains, out_own, out_other)
+    n1 = swap_core(n0)
+    s1 = swap_core(s0)
+
+    hid, dg, du, down_keep, down_send, wg, wu, wd = hidden_and_back((n0, n1), (ct0, ct1), g, u, d)
+    down_in = swap_x(down_send)
+    gate_keep, gate_send, gn_own, gn_other = gate_back((n0, n1), dg, du, wg, wu)
+    gn_in = swap_core(gn_other)
+    gate_in = swap_y(gate_send)
+    mid, br0, grad_heads, gain2 = mid_back(gn_own, gn_in, resid, ct0, gains, wo)
+    ga = [grad_heads[0]] + [swap_b(grad_heads[j], j) for j in (2, 3, 1)]
+    ga = [ga[0], ga[3], ga[1], ga[2]]
+    br1 = swap_core(br0)
+    up_keep, up_send = up_out_back((n0, n1), du, (s0, s1), (br0, br1))
+    up_in = swap_y(up_send)
+
+    qkv_keep, qkv_send, gn_keep, gn_send = attend_back(
+        q, k, v, normed, attn, ga, lse, cos, sin, start, wqkv, xs, gain2)
+    qkv_in = swap_x(qkv_send)
+
+    down_2 = added(down_keep, down_in)
+    down_2in = swap_y(down_2[1])
+    grad_down = sum_z(added(down_2[0], down_2in))
+    gate_2 = added(gate_keep, gate_in)
+    gate_2in = swap_x(gate_2[1])
+    gate_rows = sum_z(added(gate_2[0], gate_2in))
+    up_2 = added(up_keep, up_in)
+    up_2in = swap_x(up_2[1])
+    up_rows = sum_z(added(up_2[0], up_2in))
+
+    own_half, other_half = down(hid, wd, resid)
+    output = (own_half + swap_core(other_half)).astype(BF)
+
+    gn_2 = added(gn_keep, swap_core(gn_send))
+    gn_2in = swap_y(gn_2[1])
+    (grad_input,) = call(last_kernel, [((256, 768), BF)], [gn_2[0], gn_2in, mid, x0, gains],
+                         flops=10_000_000, nbytes=3_000_000)
+
+    rows96 = sum_z(added(qkv_keep, qkv_in)).astype(BF).reshape(4, 24, 640)
+    order = by_index([rows96[j] for j in range(4)], b)
+    pieces = by_index([order[0]] + [swap_b(order[j], j) for j in (1, 2, 3)], b)
+    whole = [piece.astype(F32) for piece in pieces]
+    grad_query, grad_key, grad_value = (
+        jnp.concatenate([piece[:, 192 * j : 192 * j + 192] for piece in whole], axis=1) for j in range(3))
+    gain_sums = sum(piece[:, 576:578] for piece in whole)
+
+    rows48 = jnp.concatenate([gate_rows, up_rows], axis=1)
+    to_other = jnp.where(first, rows48[24:], rows48[:24])
+    to_own = jnp.where(first, rows48[:24], rows48[24:])
+    came = swap_core(to_other)
+    even, odd = jnp.where(first, to_own, came), jnp.where(first, came, to_own)
+
+    def woven(at):
+        return jnp.stack([even[:, at : at + 1024].reshape(24, 16, 64), odd[:, at : at + 1024].reshape(24, 16, 64)],
+                         axis=2).reshape(24, 2048)
+
+    grad_out = jnp.concatenate([even[:, 2048:], odd[:, 2048:]], axis=1)
+    return (output[None], grad_input[None], gain_sums[:, 0], grad_query, grad_key, grad_value, grad_out,
+            gain_sums[:, 1], woven(0), woven(1024), grad_down)
+
+
 def solution(mesh):
+    fits = dict(mesh.shape) == {"dp": 8, "blk": 4}
     return jax.shard_map(
-        shards,
+        fast_shards if fits else shards,
         mesh=mesh,
         in_specs=(
             P("dp", "blk", None),

time: 1350 us -> 313 us (0.23)
  waiting for transfers between devices: 1080 us -> 137 us
  blocking collectives: 87 us -> 5.07 us
  matrix products: 76.9 us -> 0 us
  starting transfers between devices: 0.9 us -> 68.6 us
  Pallas kernels: 0 us -> 65.9 us
  other arithmetic: 39.7 us -> 11 us
  local copies, waits for them, and re-layouts: 46.3 us -> 20.4 us
  between operations: 15.8 us -> 1.89 us
    reduce_scatter x8 -> x0, waiting for transfers between devices: 742 us -> none  [the longest x1 121 us: shards(): lax.psum_scatter(grad_up_w, ('dp', 'blk'), scatter_dimension=0, tiled=True)]
    all_gather x9 -> x0, waiting for transfers between devices: 336 us -> none  [the longest x1 58.9 us: shards(): lax.all_gather(w_up, ('dp', 'blk'), axis=0, tiled=True)]
    ppermute x0 -> x67, waiting for transfers between devices: none -> 137 us  [the longest x10 55.7 us: swap_x(): return lax.ppermute(v, 'dp', [(i, i ^ 1) for i in range(8)])]
    unnamed x2 -> x0, blocking collectives: 81.5 us -> none
    dot_general x49 -> x0, matrix products: 76.9 us -> none  [the longest x7 20.1 us: left_product(): lax.dot_general(left_matrix, right_matrix, (((0,), (0,)), ((), ())), pref...]
    ppermute x0 -> x67, starting transfers between devices: none -> 68.6 us  [the longest x24 36.7 us: swap_z(): return lax.ppermute(v, 'dp', [(i, i ^ 2 * k) for i in range(8)])]
    pallas_call x0 -> x9, Pallas kernels: none -> 65.9 us  [call(): pl.pallas_call(kernel, out_shape=[jax.ShapeDtypeStruct(shape, dtype) for...]
    dynamic_slice x32 -> x0, local copies, waits for them, and re-layouts: 24 us -> none  [the longest x8 4.8 us: attend_visit(): lax.dynamic_slice_in_dim(value_piece, offset, local_rows, 0)]
  transfers between devices with their start and end apart: 17 -> 67, of which waited for: 17 -> 30; matrix products, arithmetic and copies ran while one was open for 7% -> 6% of each run, Pallas kernels for 0% -> 18%
where the time goes in v1:
time: 313 us; the launch traced here: 310 us
  waiting for transfers between devices  137 us (44%)
  starting transfers between devices  68.6 us (22%)
  Pallas kernels  65.9 us (21%)
  local copies, waits for them, and re-layouts  20.4 us (7%)
  other arithmetic  11 us (4%)
  blocking collectives  5.07 us (2%)
    pallas_call x9, Pallas kernels, call(): pl.pallas_call(kernel, out_shape=[jax.ShapeDtypeStruct(shape, dtype) for...  65.9 us
    ppermute x10, waiting for transfers between devices, swap_x(): return lax.ppermute(v, 'dp', [(i, i ^ 1) for i in range(8)])  55.7 us
    ppermute x33, waiting for transfers between devices, swap_b(): return lax.ppermute(v, 'blk', [(i, i ^ k) for i in range(4)])  46.5 us
    ppermute x24, starting transfers between devices, swap_z(): return lax.ppermute(v, 'dp', [(i, i ^ 2 * k) for i in range(8)])  36.7 us
    ppermute x24, waiting for transfers between devices, swap_z(): return lax.ppermute(v, 'dp', [(i, i ^ 2 * k) for i in range(8)])  34.9 us
    ppermute x33, starting transfers between devices, swap_b(): return lax.ppermute(v, 'blk', [(i, i ^ k) for i in range(4)])  19.7 us
    ppermute x10, starting transfers between devices, swap_x(): return lax.ppermute(v, 'dp', [(i, i ^ 1) for i in range(8)])  12.1 us
  transfers between devices with their start and end apart: 67, of which 30 were waited for; matrix products, arithmetic and copies ran while one was open for 6% of the time, Pallas kernels for 18%

profile of v1, /device:TPU:0, one launch (start us, length us, event | category | flops | bytes accessed | tf_op | source)
XLA Modules:
  0.0 309.9 jit_solution(15185911919757859976)
XLA Ops:
  4.4 3.1 collective-permute-start.3
  7.4 2.6 collective-permute-start.4
  10.5 3.9 %collective-permute-start.31 = (bf16[64,768]{1,0:T(8,128)(2,1)}, bf16[64,768]{1,0:T(8,128)(2,1)S(1)}, u32[]{:S(2)}, u32[]{:S(2)}) collective-permute-start(bf16[64,768]{1,0:T(8,128)(2,1)} %param.24), channel_id=1, source_target_pairs={{0,24},{4,28},{8,16},{12,20},{16,8},{20,12},{24,0},{28,4},{1,25},{... | collective-permute-start | bytes 294920 | tf_op jit(solution)/shard_map/ppermute | solution.py:743
  16.8 5.1 %all-gather = s32[1,1024]{1,0:T(1,128)S(1)} all-gather(s32[1,256]{1,0:T(1,128)S(1)} %copy-done.25), channel_id=2, replica_groups=mesh['dp'=8,'blk'=4] {'blk'}, dimensions={1}, use_global_device_ids=true | all-gather | bytes 5120 | tf_op jit(solution)/shard_map/all_gather | solution.py:800
  21.9 3.2 %fusion.3 = (f32[1024,128]{1,0:T(8,128)}, f32[1024,128]{1,0:T(8,128)}) fusion(f32[128]{0:T(128)S(1)} %get-tuple-element.169, f32[128]{0:T(128)S(1)} %get-tuple-element.170, f32[1024]{0:T(1024)S(1)} %convert_element_type.171), kind=kLoop, calls=%fused_computation.18 | loop fusion | flops 262144 | bytes 1053696 | tf_op jit(solution)/shard_map/mul | solution.py:840
  28.0 4.3 %collective-permute-start.24 = (bf16[48,1024]{1,0:T(8,128)(2,1)S(1)}, bf16[48,1024]{1,0:T(8,128)(2,1)S(1)}, u32[]{:S(2)}, u32[]{:S(2)}) collective-permute-start(bf16[48,1024]{1,0:T(8,128)(2,1)S(1)} %pad_maximum_fusion.16), channel_id=1, source_target_pairs={{0,16},{4,20},{8,24},{12,28},{16,0},{20,4},{24,8},{28,12},{1,17},{... | collective-permute-start | bytes 294920 | tf_op jit(solution)/shard_map/ppermute | solution.py:743
  34.5 2.5 collective-permute-start.15
  38.4 1.8 collective-permute-done.24
  40.2 1.5 collective-permute-start.1
  41.8 1.5 collective-permute-done.14
  43.3 7.9 %collective-permute-done.15 = bf16[48,1408]{1,0:T(8,128)(2,1)S(1)} collective-permute-done((bf16[48,1408]{1,0:T(8,128)(2,1)S(1)}, bf16[48,1408]{1,0:T(8,128)(2,1)S(1)}, u32[]{:S(2)}, u32[]{:S(2)}) %collective-permute-start.15) | collective-permute-done | bytes 135200 | tf_op jit(solution)/shard_map/ppermute | solution.py:743
  53.3 3.5 %collective-permute-done.6 = bf16[4,24,640]{2,1,0:T(8,128)(2,1)S(1)} collective-permute-done((bf16[4,24,640]{2,1,0:T(8,128)(2,1)S(1)}, bf16[4,24,640]{2,1,0:T(8,128)(2,1)S(1)}, u32[]{:S(2)}, u32[]{:S(2)}) %collective-permute-start.6) | collective-permute-done | bytes 122912 | tf_op jit(solution)/shard_map/ppermute | solution.py:751
  60.8 10.3 %collective-permute-done.18.refs_2_ = bf16[4,48,1408]{2,1,0:T(8,128)(2,1)S(1)} collective-permute-done((bf16[4,48,1408]{2,1,0:T(8,128)(2,1)S(1)}, bf16[4,48,1408]{2,1,0:T(8,128)(2,1)S(1)}, u32[]{:S(2)}, u32[]{:S(2)}) %collective-permute-start.18) | collective-permute-done | bytes 540704 | tf_op jit(solution)/shard_map/ppermute | solution.py:747
  72.3 1.6 collective-permute-start.9
  74.9 10.6 %collective-permute-done.19.refs_3_ = bf16[4,48,1408]{2,1,0:T(8,128)(2,1)S(1)} collective-permute-done((bf16[4,48,1408]{2,1,0:T(8,128)(2,1)S(1)}, bf16[4,48,1408]{2,1,0:T(8,128)(2,1)S(1)}, u32[]{:S(2)}, u32[]{:S(2)}) %collective-permute-start.19) | collective-permute-done | bytes 540704 | tf_op jit(solution)/shard_map/ppermute | solution.py:751
  88.7 10.4 %shard_map.203 = (bf16[1024,256]{1,0:T(8,128)(2,1)}, bf16[1024,256]{1,0:T(8,128)(2,1)}, bf16[1024,256]{1,0:T(8,128)(2,1)}, bf16[1024,768]{1,0:T(8,128)(2,1)}, bf...) custom-call(bf16[256,768]{1,0:T(8,128)(2,1)} %bitcast.157, ...), custom_call_target="tpu_custom_call" | custom-call | flops 4000000000 | bytes 8000000 | tf_op jit(solution)/shard_map/pallas_call | solution.py:367
  99.1 1.8 slice_bitcast_fusion.20
  102.3 2.1 collective-permute-done.26.refs_5_
  104.4 1.6 collective-permute-start.33
  108.5 1.5 collective-permute-done.12.a3
  110.0 1.5 collective-permute-start.34
  112.3 4.7 %shard_map.204 = (f32[256,768]{1,0:T(8,128)}, bf16[256,768]{1,0:T(8,128)(2,1)}, bf16[4,256,256]{2,1,0:T(8,128)(2,1)}, bf16[2,768,384]{2,1,0:T(8,128)(2,1)}) custom-call(bf16[256,256]{1,0:T(8,128)(2,1)} %get-tuple-element.102.a0, bf16[256,256]{1,0:T(8,128)(2,1)} %copy-done.16, bf16[256,256]{1,0:T(8,128)(2,1)} %copy-done.17, bf16[256,256]{1,0:T(8,128)(2,1)} %copy-done.18, ...), custom_call_target="tpu_custom_call" | custom-call | flops 400000000 | bytes 4000000 | tf_op jit(solution)/shard_map/pallas_call | solution.py:367
  117.2 7.5 %collective-permute-done.27.refs_6_ = bf16[4,48,1024]{2,1,0:T(8,128)(2,1)S(1)} collective-permute-done((bf16[4,48,1024]{2,1,0:T(8,128)(2,1)S(1)}, bf16[4,48,1024]{2,1,0:T(8,128)(2,1)S(1)}, u32[]{:S(2)}, u32[]{:S(2)}) %collective-permute-start.27) | collective-permute-done | bytes 393248 | tf_op jit(solution)/shard_map/ppermute | solution.py:747
  124.6 8.4 %collective-permute-done.34.refs_11_ = bf16[4,64,768]{2,1,0:T(8,128)(2,1)S(1)} collective-permute-done((bf16[4,64,768]{2,1,0:T(8,128)(2,1)}, bf16[4,64,768]{2,1,0:T(8,128)(2,1)S(1)}, u32[]{:S(2)}, u32[]{:S(2)}) %collective-permute-start.34) | collective-permute-done | bytes 393248 | tf_op jit(solution)/shard_map/ppermute | solution.py:747
  133.0 8.4 %collective-permute-done.28.refs_7_ = bf16[4,48,1024]{2,1,0:T(8,128)(2,1)S(1)} collective-permute-done((bf16[4,48,1024]{2,1,0:T(8,128)(2,1)}, bf16[4,48,1024]{2,1,0:T(8,128)(2,1)S(1)}, u32[]{:S(2)}, u32[]{:S(2)}) %collective-permute-start.28) | collective-permute-done | bytes 393248 | tf_op jit(solution)/shard_map/ppermute | solution.py:747
  143.0 10.7 %shard_map.205 = (bf16[512,1024]{1,0:T(8,128)(2,1)}, bf16[512,1024]{1,0:T(8,128)(2,1)}, bf16[512,1024]{1,0:T(8,128)(2,1)}, bf16[2,4,64,768]{3,2,1,0:T(8,128)(2,1...) custom-call(bf16[256,768]{1,0:T(8,128)(2,1)} %get-tuple-element.49.n, ...), custom_call_target="tpu_custom_call" | custom-call | flops 3300000000 | bytes 12000000 | tf_op jit(solution)/shard_map/pallas_call | solution.py:367
  153.7 1.5 collective-permute-start.62
  155.2 6.4 %shard_map.207 = (bf16[2,4,48,1024]{3,2,1,0:T(8,128)(2,1)}, bf16[2,4,48,1024]{3,2,1,0:T(8,128)(2,1)}, f32[256,768]{1,0:T(8,128)}, f32[256,768]{1,0:T(8,128)}) custom-call(bf16[256,768]{1,0:T(8,128)(2,1)} %get-tuple-element.49.n0, bf16[256,768]{1,0:T(8,128)(2,1)} %copy-done.33, bf16[512,1024]{1,0:T(8,128)(2,1)} %get-tuple-element.59.dg, ...), custom_call_target="tpu_custom_call" | custom-call | flops 2500000000 | bytes 9000000 | tf_op jit(solution)/shard_map/pallas_call | solution.py:367
  163.6 3.9 %shard_map.206 = (f32[256,768]{1,0:T(8,128)}, f32[256,768]{1,0:T(8,128)}) custom-call(bf16[512,1024]{1,0:T(8,128)(2,1)} %get-tuple-element.50.hid, bf16[1024,768]{1,0:T(8,128)(2,1)} %get-tuple-element.51.wd, f32[256,768]{1,0:T(8,128)} %get-tuple-element.52.resid), custom_call_target="tpu_custom_call" | custom-call | flops 800000000 | bytes 5000000 | tf_op jit(solution)/shard_map/pallas_call | solution.py:367
  167.6 5.9 %collective-permute-done.62 = bf16[2,4,64,768]{3,2,1,0:T(8,128)(2,1)S(1)} collective-permute-done((bf16[2,4,64,768]{3,2,1,0:T(8,128)(2,1)}, bf16[2,4,64,768]{3,2,1,0:T(8,128)(2,1)S(1)}, u32[]{:S(2)}, u32[]{:S(2)}) %collective-permute-start.62) | collective-permute-done | bytes 786464 | tf_op jit(solution)/shard_map/ppermute | solution.py:747
  176.0 4.1 %shard_map.208 = (f32[256,768]{1,0:T(8,128)}, bf16[256,768]{1,0:T(8,128)(2,1)}, bf16[4,256,256]{2,1,0:T(8,128)(2,1)}, f32[8,768]{1,0:T(8,128)}) custom-call(f32[256,768]{1,0:T(8,128)} %get-tuple-element.63.gn_own, f32[256,768]{1,0:T(8,128)} %copy-done.8, f32[256,768]{1,0:T(8,128)} %get-tuple-element.52.resid, bf16[256,768]{1,0:T(8,128)(2,1)} %bitcast.169, ...), custom_call_target="tpu_custom_call" | custom-call | flops 400000000 | bytes 5000000 | tf_op jit(solution)/shard_map/pallas_call | solution.py:367
  180.1 1.9 slice_bitcast_fusion.16
  186.7 7.4 %collective-permute-done.38.g2 = bf16[256,256]{1,0:T(8,128)(2,1)S(1)} collective-permute-done((bf16[256,256]{1,0:T(8,128)(2,1)S(1)}, bf16[256,256]{1,0:T(8,128)(2,1)S(1)}, u32[]{:S(2)}, u32[]{:S(2)}) %collective-permute-start.38) | collective-permute-done | bytes 131104 | tf_op jit(solution)/shard_map/ppermute | solution.py:751
  195.7 18.1 %shard_map.209 = (bf16[4,96,640]{2,1,0:T(8,128)(2,1)}, bf16[4,96,640]{2,1,0:T(8,128)(2,1)}, bf16[2,256,768]{2,1,0:T(8,128)(2,1)}, bf16[2,256,768]{2,1,0:T(8,128)(2,1)}) custom-call(bf16[1024,256]{1,0:T(8,128)(2,1)} %get-tuple-element.55.q, bf16[1024,256]{1,0:T(8,128)(2,1)} %get-tuple-element.56.k, bf16[1024,256]{1,0:T(8,128)(2,1)} %get-tuple-element.57.v, ...), custom_call_target="tpu_custom_call" | custom-call | flops 10000000000 | bytes 12000000 | tf_op jit(solution)/shard_map/pallas_call | solution.py:367
  215.4 2.9 collective-permute-start.65
  218.3 5.0 %shard_map.211 = (bf16[2,4,48,1408]{3,2,1,0:T(8,128)(2,1)}, bf16[2,4,48,1408]{3,2,1,0:T(8,128)(2,1)}) custom-call(bf16[256,768]{1,0:T(8,128)(2,1)} %get-tuple-element.49.n0, bf16[256,768]{1,0:T(8,128)(2,1)} %copy-done.33, bf16[512,1024]{1,0:T(8,128)(2,1)} %get-tuple-element.60.du, bf16[4,256,256]{2,1,0:T(8,128)(2,1)} %get-tuple-element.77.s0, ...), custom_call_target="tpu_custom_call" | custom-call | flops 1200000000 | bytes 8000000 | tf_op jit(solution)/shard_map/pallas_call | solution.py:367
  225.0 3.1 %collective-permute-done.42 = bf16[4,96,640]{2,1,0:T(8,128)(2,1)S(1)} collective-permute-done((bf16[4,96,640]{2,1,0:T(8,128)(2,1)}, bf16[4,96,640]{2,1,0:T(8,128)(2,1)S(1)}, u32[]{:S(2)}, u32[]{:S(2)}) %collective-permute-start.42) | collective-permute-done | bytes 491552 | tf_op jit(solution)/shard_map/ppermute | solution.py:747
  228.3 2.1 collective-permute-start.43
  231.2 1.7 collective-permute-start.45
  233.6 3.9 %collective-permute-done.43 = bf16[96,640]{1,0:T(8,128)(2,1)S(1)} collective-permute-done((bf16[96,640]{1,0:T(8,128)(2,1)S(1)}, bf16[96,640]{1,0:T(8,128)(2,1)S(1)}, u32[]{:S(2)}, u32[]{:S(2)}) %collective-permute-start.43) | collective-permute-done | bytes 122912 | tf_op jit(solution)/shard_map/ppermute | solution.py:743
  237.5 8.5 %collective-permute-done.44 = bf16[96,640]{1,0:T(8,128)(2,1)S(1)} collective-permute-done((bf16[96,640]{1,0:T(8,128)(2,1)S(1)}, bf16[96,640]{1,0:T(8,128)(2,1)S(1)}, u32[]{:S(2)}, u32[]{:S(2)}) %collective-permute-start.44) | collective-permute-done | bytes 122912 | tf_op jit(solution)/shard_map/ppermute | solution.py:743
  246.0 2.1 collective-permute-start.53
  252.5 13.9 %collective-permute-done.46 = bf16[24,640]{1,0:T(8,128)(2,1)S(1)} collective-permute-done((bf16[24,640]{1,0:T(8,128)(2,1)S(1)}, bf16[24,640]{1,0:T(8,128)(2,1)S(1)}, u32[]{:S(2)}, u32[]{:S(2)}) %collective-permute-start.46) | collective-permute-done | bytes 30752 | tf_op jit(solution)/shard_map/ppermute | solution.py:751
  270.3 12.0 %collective-permute-done.57 = bf16[4,48,1408]{2,1,0:T(8,128)(2,1)S(1)} collective-permute-done((bf16[4,48,1408]{2,1,0:T(8,128)(2,1)S(1)}, bf16[4,48,1408]{2,1,0:T(8,128)(2,1)S(1)}, u32[]{:S(2)}, u32[]{:S(2)}) %collective-permute-start.57) | collective-permute-done | bytes 540704 | tf_op jit(solution)/shard_map/ppermute | solution.py:747
  282.6 5.5 %collective-permute-start.58 = (bf16[48,1408]{1,0:T(8,128)(2,1)S(1)}, bf16[48,1408]{1,0:T(8,128)(2,1)S(1)}, u32[]{:S(2)}, u32[]{:S(2)}) collective-permute-start(bf16[48,1408]{1,0:T(8,128)(2,1)S(1)} %get-tuple-element.92), channel_id=1, source_target_pairs={{0,8},{4,12},{8,0},{12,4},{16,24},{20,28},{24,16},{28,20},{1,9},{5... | collective-permute-start | bytes 405512 | tf_op jit(solution)/shard_map/ppermute | solution.py:743
  289.0 1.5 collective-permute-start.60
  292.8 7.3 %collective-permute-done.59 = bf16[48,1408]{1,0:T(8,128)(2,1)S(1)} collective-permute-done((bf16[48,1408]{1,0:T(8,128)(2,1)S(1)}, bf16[48,1408]{1,0:T(8,128)(2,1)S(1)}, u32[]{:S(2)}, u32[]{:S(2)}) %collective-permute-start.59) | collective-permute-done | bytes 135200 | tf_op jit(solution)/shard_map/ppermute | solution.py:743
  303.1 2.6 shard_map.210
  (286 shorter events, 64.8 us)
Async XLA Ops:
  4.4 28.0 %collective-permute-start.3 = (bf16[4,24,640]{2,1,0:T(8,128)(2,1)S(1)}, bf16[4,24,640]{2,1,0:T(8,128)(2,1)S(1)}, u32[]{:S(2)}, u32[]{:S(2)}) collective-permute-start(bf16[4,24,640]{2,1,0:T(8,128)(2,1)S(1)} %fusion.17), channel_id=1, source_target_pairs={{0,8},{4,12},{8,0},{12,4},{16,24},{20,28},{24,16},{28,20},{1,9},{5... | collective-permute-start | bytes 368648 | tf_op jit(solution)/shard_map/ppermute | solution.py:743
  7.4 25.0 %collective-permute-start.4 = (bf16[4,24,640]{2,1,0:T(8,128)(2,1)S(1)}, bf16[4,24,640]{2,1,0:T(8,128)(2,1)S(1)}, u32[]{:S(2)}, u32[]{:S(2)}) collective-permute-start(bf16[4,24,640]{2,1,0:T(8,128)(2,1)S(1)} %fusion.17), channel_id=1, source_target_pairs={{0,16},{4,20},{8,24},{12,28},{16,0},{20,4},{24,8},{28,12},{1,17},{... | collective-permute-start | bytes 368648 | tf_op jit(solution)/shard_map/ppermute | solution.py:743
  10.0 16.4 %collective-permute-start.29 = (bf16[64,768]{1,0:T(8,128)(2,1)}, bf16[64,768]{1,0:T(8,128)(2,1)S(1)}, u32[]{:S(2)}, u32[]{:S(2)}) collective-permute-start(bf16[64,768]{1,0:T(8,128)(2,1)} %param.24), channel_id=1, source_target_pairs={{0,8},{4,12},{8,0},{12,4},{16,24},{20,28},{24,16},{28,20},{1,9},{5... | collective-permute-start | bytes 294920 | tf_op jit(solution)/shard_map/ppermute | solution.py:743
  10.5 16.0 %collective-permute-start.30 = (bf16[64,768]{1,0:T(8,128)(2,1)}, bf16[64,768]{1,0:T(8,128)(2,1)S(1)}, u32[]{:S(2)}, u32[]{:S(2)}) collective-permute-start(bf16[64,768]{1,0:T(8,128)(2,1)} %param.24), channel_id=1, source_target_pairs={{0,16},{4,20},{8,24},{12,28},{16,0},{20,4},{24,8},{28,12},{1,17},{... | collective-permute-start | bytes 294920 | tf_op jit(solution)/shard_map/ppermute | solution.py:743
  10.5 16.4 %collective-permute-start.31 = (bf16[64,768]{1,0:T(8,128)(2,1)}, bf16[64,768]{1,0:T(8,128)(2,1)S(1)}, u32[]{:S(2)}, u32[]{:S(2)}) collective-permute-start(bf16[64,768]{1,0:T(8,128)(2,1)} %param.24), channel_id=1, source_target_pairs={{0,24},{4,28},{8,16},{12,20},{16,8},{20,12},{24,0},{28,4},{1,25},{... | collective-permute-start | bytes 294920 | tf_op jit(solution)/shard_map/ppermute | solution.py:743
  28.0 12.2 %collective-permute-start.24 = (bf16[48,1024]{1,0:T(8,128)(2,1)S(1)}, bf16[48,1024]{1,0:T(8,128)(2,1)S(1)}, u32[]{:S(2)}, u32[]{:S(2)}) collective-permute-start(bf16[48,1024]{1,0:T(8,128)(2,1)S(1)} %pad_maximum_fusion.16), channel_id=1, source_target_pairs={{0,16},{4,20},{8,24},{12,28},{16,0},{20,4},{24,8},{28,12},{1,17},{... | collective-permute-start | bytes 294920 | tf_op jit(solution)/shard_map/ppermute | solution.py:743
  34.5 16.8 %collective-permute-start.15 = (bf16[48,1408]{1,0:T(8,128)(2,1)S(1)}, bf16[48,1408]{1,0:T(8,128)(2,1)S(1)}, u32[]{:S(2)}, u32[]{:S(2)}) collective-permute-start(bf16[48,1408]{1,0:T(8,128)(2,1)S(1)} %fusion.15), channel_id=1, source_target_pairs={{0,16},{4,20},{8,24},{12,28},{16,0},{20,4},{24,8},{28,12},{1,17},{... | collective-permute-start | bytes 405512 | tf_op jit(solution)/shard_map/ppermute | solution.py:743
  38.4 13.6 %collective-permute-start.16 = (bf16[48,1408]{1,0:T(8,128)(2,1)S(1)}, bf16[48,1408]{1,0:T(8,128)(2,1)S(1)}, u32[]{:S(2)}, u32[]{:S(2)}) collective-permute-start(bf16[48,1408]{1,0:T(8,128)(2,1)S(1)} %fusion.15), channel_id=1, source_target_pairs={{0,24},{4,28},{8,16},{12,20},{16,8},{20,12},{24,0},{28,4},{1,25},{... | collective-permute-start | bytes 405512 | tf_op jit(solution)/shard_map/ppermute | solution.py:743
  40.2 32.0 %collective-permute-start.1 = (bf16[256,768]{1,0:T(8,128)(2,1)S(1)}, bf16[256,768]{1,0:T(8,128)(2,1)S(1)}, u32[]{:S(2)}, u32[]{:S(2)}) collective-permute-start(bf16[256,768]{1,0:T(8,128)(2,1)S(1)} %bitcast.161), channel_id=1, source_target_pairs={{0,2},{1,3},{2,0},{3,1},{4,6},{5,7},{6,4},{7,5},{8,10},{9,11},{10,... | collective-permute-start | bytes 1179656 | tf_op jit(solution)/shard_map/ppermute | solution.py:751
  41.7 45.0 %collective-permute-start = (bf16[256,768]{1,0:T(8,128)(2,1)S(1)}, bf16[256,768]{1,0:T(8,128)(2,1)S(1)}, u32[]{:S(2)}, u32[]{:S(2)}) collective-permute-start(bf16[256,768]{1,0:T(8,128)(2,1)S(1)} %bitcast.162), channel_id=1, source_target_pairs={{0,1},{1,0},{2,3},{3,2},{4,5},{5,4},{6,7},{7,6},{8,9},{9,8},{10,11... | collective-permute-start | bytes 1179656 | tf_op jit(solution)/shard_map/ppermute | solution.py:751
  53.0 64.1 %collective-permute-start.22 = (bf16[256,768]{1,0:T(8,128)(2,1)S(1)}, bf16[256,768]{1,0:T(8,128)(2,1)S(1)}, u32[]{:S(2)}, u32[]{:S(2)}) collective-permute-start(bf16[256,768]{1,0:T(8,128)(2,1)S(1)} %bitcast.170), channel_id=1, source_target_pairs={{0,1},{1,0},{2,3},{3,2},{4,5},{5,4},{6,7},{7,6},{8,9},{9,8},{10,11... | collective-permute-start | bytes 1179656 | tf_op jit(solution)/shard_map/ppermute | solution.py:751
  56.8 14.3 %collective-permute-start.18 = (bf16[4,48,1408]{2,1,0:T(8,128)(2,1)S(1)}, bf16[4,48,1408]{2,1,0:T(8,128)(2,1)S(1)}, u32[]{:S(2)}, u32[]{:S(2)}) collective-permute-start(bf16[4,48,1408]{2,1,0:T(8,128)(2,1)S(1)} %pad_maximum_fusion.1.refs_0_), channel_id=1, source_target_pairs={{0,4},{4,0},{8,12},{12,8},{16,20},{20,16},{24,28},{28,24},{1,5},{5... | collective-permute-start | bytes 1622024 | tf_op jit(solution)/shard_map/ppermute | solution.py:747
  59.7 15.2 %collective-permute-start.17 = (bf16[4,48,1408]{2,1,0:T(8,128)(2,1)S(1)}, bf16[4,48,1408]{2,1,0:T(8,128)(2,1)S(1)}, u32[]{:S(2)}, u32[]{:S(2)}) collective-permute-start(bf16[4,48,1408]{2,1,0:T(8,128)(2,1)S(1)} %pad_maximum_fusion.1.refs_0_), channel_id=1, source_target_pairs={{0,2},{1,3},{2,0},{3,1},{4,6},{5,7},{6,4},{7,5},{8,10},{9,11},{10,... | collective-permute-start | bytes 1622024 | tf_op jit(solution)/shard_map/ppermute | solution.py:751
  71.1 14.4 %collective-permute-start.19 = (bf16[4,48,1408]{2,1,0:T(8,128)(2,1)S(1)}, bf16[4,48,1408]{2,1,0:T(8,128)(2,1)S(1)}, u32[]{:S(2)}, u32[]{:S(2)}) collective-permute-start(bf16[4,48,1408]{2,1,0:T(8,128)(2,1)S(1)} %collective-permute-done.18.refs_2_), channel_id=1, source_target_pairs={{0,2},{1,3},{2,0},{3,1},{4,6},{5,7},{6,4},{7,5},{8,10},{9,11},{10,... | collective-permute-start | bytes 1622024 | tf_op jit(solution)/shard_map/ppermute | solution.py:751
  72.3 15.5 %collective-permute-start.9 = (bf16[4,96,640]{2,1,0:T(8,128)(2,1)S(1)}, bf16[4,96,640]{2,1,0:T(8,128)(2,1)S(1)}, u32[]{:S(2)}, u32[]{:S(2)}) collective-permute-start(bf16[4,96,640]{2,1,0:T(8,128)(2,1)S(1)} %bitcast.164), channel_id=1, source_target_pairs={{0,4},{4,0},{8,12},{12,8},{16,20},{20,16},{24,28},{28,24},{1,5},{5... | collective-permute-start | bytes 1474568 | tf_op jit(solution)/shard_map/ppermute | solution.py:747
  74.9 12.9 %collective-permute-start.2 = (bf16[256,768]{1,0:T(8,128)(2,1)S(1)}, bf16[256,768]{1,0:T(8,128)(2,1)S(1)}, u32[]{:S(2)}, u32[]{:S(2)}) collective-permute-start(bf16[256,768]{1,0:T(8,128)(2,1)S(1)} %collective-permute-done.1.x2), channel_id=1, source_target_pairs={{0,1},{1,0},{2,3},{3,2},{4,5},{5,4},{6,7},{7,6},{8,9},{9,8},{10,11... | collective-permute-start | bytes 1179656 | tf_op jit(solution)/shard_map/ppermute | solution.py:751
  85.5 15.7 %collective-permute-start.32 = (bf16[4,64,768]{2,1,0:T(8,128)(2,1)S(1)}, bf16[4,64,768]{2,1,0:T(8,128)(2,1)}, u32[]{:S(2)}, u32[]{:S(2)}) collective-permute-start(bf16[4,64,768]{2,1,0:T(8,128)(2,1)S(1)} %pad_maximum_fusion.4.refs_8_), channel_id=1, source_target_pairs={{0,2},{1,3},{2,0},{3,1},{4,6},{5,7},{6,4},{7,5},{8,10},{9,11},{10,... | collective-permute-start | bytes 1179656 | tf_op jit(solution)/shard_map/ppermute | solution.py:751
  86.8 17.6 %collective-permute-start.26 = (bf16[4,48,1024]{2,1,0:T(8,128)(2,1)S(1)}, bf16[4,48,1024]{2,1,0:T(8,128)(2,1)}, u32[]{:S(2)}, u32[]{:S(2)}) collective-permute-start(bf16[4,48,1024]{2,1,0:T(8,128)(2,1)S(1)} %pad_maximum_fusion.3.refs_4_), channel_id=1, source_target_pairs={{0,2},{1,3},{2,0},{3,1},{4,6},{5,7},{6,4},{7,5},{8,10},{9,11},{10,... | collective-permute-start | bytes 1179656 | tf_op jit(solution)/shard_map/ppermute | solution.py:751
  87.8 23.7 %collective-permute-start.20 = (bf16[4,4,48,384]{3,2,1,0:T(8,128)(2,1)S(1)}, bf16[4,4,48,384]{3,2,1,0:T(8,128)(2,1)S(1)}, u32[]{:S(2)}, u32[]{:S(2)}) collective-permute-start(bf16[4,4,48,384]{3,2,1,0:T(8,128)(2,1)S(1)} %pad_maximum_fusion.own), channel_id=1, source_target_pairs={{0,1},{1,0},{2,3},{3,2},{4,5},{5,4},{6,7},{7,6},{8,9},{9,8},{10,11... | collective-permute-start | bytes 1769480 | tf_op jit(solution)/shard_map/ppermute | solution.py:751
  104.4 12.7 %collective-permute-start.33 = (bf16[4,64,768]{2,1,0:T(8,128)(2,1)S(1)}, bf16[4,64,768]{2,1,0:T(8,128)(2,1)S(1)}, u32[]{:S(2)}, u32[]{:S(2)}) collective-permute-start(bf16[4,64,768]{2,1,0:T(8,128)(2,1)S(1)} %pad_maximum_fusion.4.refs_8_), channel_id=1, source_target_pairs={{0,4},{4,0},{8,12},{12,8},{16,20},{20,16},{24,28},{28,24},{1,5},{5... | collective-permute-start | bytes 1179656 | tf_op jit(solution)/shard_map/ppermute | solution.py:747
  107.0 17.6 %collective-permute-start.27 = (bf16[4,48,1024]{2,1,0:T(8,128)(2,1)S(1)}, bf16[4,48,1024]{2,1,0:T(8,128)(2,1)S(1)}, u32[]{:S(2)}, u32[]{:S(2)}) collective-permute-start(bf16[4,48,1024]{2,1,0:T(8,128)(2,1)S(1)} %pad_maximum_fusion.3.refs_4_), channel_id=1, source_target_pairs={{0,4},{4,0},{8,12},{12,8},{16,20},{20,16},{24,28},{28,24},{1,5},{5... | collective-permute-start | bytes 1179656 | tf_op jit(solution)/shard_map/ppermute | solution.py:747
  110.0 23.0 %collective-permute-start.34 = (bf16[4,64,768]{2,1,0:T(8,128)(2,1)}, bf16[4,64,768]{2,1,0:T(8,128)(2,1)S(1)}, u32[]{:S(2)}, u32[]{:S(2)}) collective-permute-start(bf16[4,64,768]{2,1,0:T(8,128)(2,1)} %collective-permute-done.32.refs_9_), channel_id=1, source_target_pairs={{0,4},{4,0},{8,12},{12,8},{16,20},{20,16},{24,28},{28,24},{1,5},{5... | collective-permute-start | bytes 1179656 | tf_op jit(solution)/shard_map/ppermute | solution.py:747
  111.5 30.0 %collective-permute-start.28 = (bf16[4,48,1024]{2,1,0:T(8,128)(2,1)}, bf16[4,48,1024]{2,1,0:T(8,128)(2,1)S(1)}, u32[]{:S(2)}, u32[]{:S(2)}) collective-permute-start(bf16[4,48,1024]{2,1,0:T(8,128)(2,1)} %collective-permute-done.26.refs_5_), channel_id=1, source_target_pairs={{0,4},{4,0},{8,12},{12,8},{16,20},{20,16},{24,28},{28,24},{1,5},{5... | collective-permute-start | bytes 1179656 | tf_op jit(solution)/shard_map/ppermute | solution.py:747
  117.1 24.4 %collective-permute-start.21 = (bf16[256,768]{1,0:T(8,128)(2,1)}, bf16[256,768]{1,0:T(8,128)(2,1)S(1)}, u32[]{:S(2)}, u32[]{:S(2)}) collective-permute-start(bf16[256,768]{1,0:T(8,128)(2,1)} %get-tuple-element.49.n0), channel_id=1, source_target_pairs={{0,1},{1,0},{2,3},{3,2},{4,5},{5,4},{6,7},{7,6},{8,9},{9,8},{10,11... | collective-permute-start | bytes 1179656 | tf_op jit(solution)/shard_map/ppermute | solution.py:751
  153.7 19.8 %collective-permute-start.62 = (bf16[2,4,64,768]{3,2,1,0:T(8,128)(2,1)}, bf16[2,4,64,768]{3,2,1,0:T(8,128)(2,1)S(1)}, u32[]{:S(2)}, u32[]{:S(2)}) collective-permute-start(bf16[2,4,64,768]{3,2,1,0:T(8,128)(2,1)} %get-tuple-element.82), channel_id=1, source_target_pairs={{0,4},{4,0},{8,12},{12,8},{16,20},{20,16},{24,28},{28,24},{1,5},{5... | collective-permute-start | bytes 2359304 | tf_op jit(solution)/shard_map/ppermute | solution.py:747
  161.7 13.5 %collective-permute-start.36 = (f32[256,768]{1,0:T(8,128)}, f32[256,768]{1,0:T(8,128)S(1)}, u32[]{:S(2)}, u32[]{:S(2)}) collective-permute-start(f32[256,768]{1,0:T(8,128)} %get-tuple-element.64), channel_id=1, source_target_pairs={{0,1},{1,0},{2,3},{3,2},{4,5},{5,4},{6,7},{7,6},{8,9},{9,8},{10,11... | collective-permute-start | bytes 2359304 | tf_op jit(solution)/shard_map/ppermute | solution.py:751
  161.7 53.6 %collective-permute-start.54 = (bf16[4,256,256]{2,1,0:T(8,128)(2,1)S(1)}, bf16[4,256,256]{2,1,0:T(8,128)(2,1)S(1)}, u32[]{:S(2)}, u32[]{:S(2)}) collective-permute-start(bf16[4,256,256]{2,1,0:T(8,128)(2,1)S(1)} %copy-done.27), channel_id=1, source_target_pairs={{0,1},{1,0},{2,3},{3,2},{4,5},{5,4},{6,7},{7,6},{8,9},{9,8},{10,11... | collective-permute-start | bytes 1572872 | tf_op jit(solution)/shard_map/ppermute | solution.py:751
  162.2 20.6 %collective-permute-start.49 = (bf16[2,4,48,1024]{3,2,1,0:T(8,128)(2,1)}, bf16[2,4,48,1024]{3,2,1,0:T(8,128)(2,1)S(1)}, u32[]{:S(2)}, u32[]{:S(2)}) collective-permute-start(bf16[2,4,48,1024]{3,2,1,0:T(8,128)(2,1)} %get-tuple-element.76), channel_id=1, source_target_pairs={{0,2},{1,3},{2,0},{3,1},{4,6},{5,7},{6,4},{7,5},{8,10},{9,11},{10,... | collective-permute-start | bytes 2359304 | tf_op jit(solution)/shard_map/ppermute | solution.py:751
  167.6 17.1 %collective-permute-start.35 = (f32[256,768]{1,0:T(8,128)}, f32[256,768]{1,0:T(8,128)S(1)}, u32[]{:S(2)}, u32[]{:S(2)}) collective-permute-start(f32[256,768]{1,0:T(8,128)} %get-tuple-element.54), channel_id=1, source_target_pairs={{0,1},{1,0},{2,3},{3,2},{4,5},{5,4},{6,7},{7,6},{8,9},{9,8},{10,11... | collective-permute-start | bytes 2359304 | tf_op jit(solution)/shard_map/ppermute | solution.py:751
  173.7 40.7 %collective-permute-start.63 = (bf16[4,64,768]{2,1,0:T(8,128)(2,1)S(1)}, bf16[4,64,768]{2,1,0:T(8,128)(2,1)S(1)}, u32[]{:S(2)}, u32[]{:S(2)}) collective-permute-start(bf16[4,64,768]{2,1,0:T(8,128)(2,1)S(1)} %slice_bitcast_fusion.2), channel_id=1, source_target_pairs={{0,2},{1,3},{2,0},{3,1},{4,6},{5,7},{6,4},{7,5},{8,10},{9,11},{10,... | collective-permute-start | bytes 1179656 | tf_op jit(solution)/shard_map/ppermute | solution.py:751
  182.8 11.2 %collective-permute-start.38 = (bf16[256,256]{1,0:T(8,128)(2,1)S(1)}, bf16[256,256]{1,0:T(8,128)(2,1)S(1)}, u32[]{:S(2)}, u32[]{:S(2)}) collective-permute-start(bf16[256,256]{1,0:T(8,128)(2,1)S(1)} %get-tuple-element.96), channel_id=1, source_target_pairs={{0,2},{1,3},{2,0},{3,1},{4,6},{5,7},{6,4},{7,5},{8,10},{9,11},{10,... | collective-permute-start | bytes 393224 | tf_op jit(solution)/shard_map/ppermute | solution.py:751
  185.6 37.7 %collective-permute-start.50 = (bf16[4,48,1024]{2,1,0:T(8,128)(2,1)S(1)}, bf16[4,48,1024]{2,1,0:T(8,128)(2,1)S(1)}, u32[]{:S(2)}, u32[]{:S(2)}) collective-permute-start(bf16[4,48,1024]{2,1,0:T(8,128)(2,1)S(1)} %slice_bitcast_fusion.4), channel_id=1, source_target_pairs={{0,4},{4,0},{8,12},{12,8},{16,20},{20,16},{24,28},{28,24},{1,5},{5... | collective-permute-start | bytes 1179656 | tf_op jit(solution)/shard_map/ppermute | solution.py:747
  194.0 21.3 %collective-permute-start.55 = (bf16[256,768]{1,0:T(8,128)(2,1)S(1)}, bf16[256,768]{1,0:T(8,128)(2,1)S(1)}, u32[]{:S(2)}, u32[]{:S(2)}) collective-permute-start(bf16[256,768]{1,0:T(8,128)(2,1)S(1)} %copy-done.35), channel_id=1, source_target_pairs={{0,1},{1,0},{2,3},{3,2},{4,5},{5,4},{6,7},{7,6},{8,9},{9,8},{10,11... | collective-permute-start | bytes 1179656 | tf_op jit(solution)/shard_map/ppermute | solution.py:751
  213.8 14.3 %collective-permute-start.42 = (bf16[4,96,640]{2,1,0:T(8,128)(2,1)}, bf16[4,96,640]{2,1,0:T(8,128)(2,1)S(1)}, u32[]{:S(2)}, u32[]{:S(2)}) collective-permute-start(bf16[4,96,640]{2,1,0:T(8,128)(2,1)} %get-tuple-element.74), channel_id=1, source_target_pairs={{0,4},{4,0},{8,12},{12,8},{16,20},{20,16},{24,28},{28,24},{1,5},{5... | collective-permute-start | bytes 1474568 | tf_op jit(solution)/shard_map/ppermute | solution.py:747
  214.4 55.7 %collective-permute-start.40 = (bf16[2,256,768]{2,1,0:T(8,128)(2,1)}, bf16[2,256,768]{2,1,0:T(8,128)(2,1)S(1)}, u32[]{:S(2)}, u32[]{:S(2)}) collective-permute-start(bf16[2,256,768]{2,1,0:T(8,128)(2,1)} %get-tuple-element.71), channel_id=1, source_target_pairs={{0,1},{1,0},{2,3},{3,2},{4,5},{5,4},{6,7},{7,6},{8,9},{9,8},{10,11... | collective-permute-start | bytes 2359304 | tf_op jit(solution)/shard_map/ppermute | solution.py:751
  215.3 13.0 %collective-permute-start.64 = (bf16[64,768]{1,0:T(8,128)(2,1)S(1)}, bf16[64,768]{1,0:T(8,128)(2,1)S(1)}, u32[]{:S(2)}, u32[]{:S(2)}) collective-permute-start(bf16[64,768]{1,0:T(8,128)(2,1)S(1)} %get-tuple-element.109), channel_id=1, source_target_pairs={{0,8},{4,12},{8,0},{12,4},{16,24},{20,28},{24,16},{28,20},{1,9},{5... | collective-permute-start | bytes 294920 | tf_op jit(solution)/shard_map/ppermute | solution.py:743
  215.4 15.0 %collective-permute-start.65 = (bf16[64,768]{1,0:T(8,128)(2,1)S(1)}, bf16[64,768]{1,0:T(8,128)(2,1)S(1)}, u32[]{:S(2)}, u32[]{:S(2)}) collective-permute-start(bf16[64,768]{1,0:T(8,128)(2,1)S(1)} %get-tuple-element.111), channel_id=1, source_target_pairs={{0,16},{4,20},{8,24},{12,28},{16,0},{20,4},{24,8},{28,12},{1,17},{... | collective-permute-start | bytes 294920 | tf_op jit(solution)/shard_map/ppermute | solution.py:743
  228.1 21.5 %collective-permute-start.51 = (bf16[48,1024]{1,0:T(8,128)(2,1)S(1)}, bf16[48,1024]{1,0:T(8,128)(2,1)S(1)}, u32[]{:S(2)}, u32[]{:S(2)}) collective-permute-start(bf16[48,1024]{1,0:T(8,128)(2,1)S(1)} %get-tuple-element.112), channel_id=1, source_target_pairs={{0,8},{4,12},{8,0},{12,4},{16,24},{20,28},{24,16},{28,20},{1,9},{5... | collective-permute-start | bytes 294920 | tf_op jit(solution)/shard_map/ppermute | solution.py:743
  230.4 15.6 %collective-permute-start.44 = (bf16[96,640]{1,0:T(8,128)(2,1)S(1)}, bf16[96,640]{1,0:T(8,128)(2,1)S(1)}, u32[]{:S(2)}, u32[]{:S(2)}) collective-permute-start(bf16[96,640]{1,0:T(8,128)(2,1)S(1)} %get-tuple-element.105), channel_id=1, source_target_pairs={{0,16},{4,20},{8,24},{12,28},{16,0},{20,4},{24,8},{28,12},{1,17},{... | collective-permute-start | bytes 368648 | tf_op jit(solution)/shard_map/ppermute | solution.py:743
  231.2 16.9 %collective-permute-start.45 = (bf16[96,640]{1,0:T(8,128)(2,1)S(1)}, bf16[96,640]{1,0:T(8,128)(2,1)S(1)}, u32[]{:S(2)}, u32[]{:S(2)}) collective-permute-start(bf16[96,640]{1,0:T(8,128)(2,1)S(1)} %get-tuple-element.104), channel_id=1, source_target_pairs={{0,24},{4,28},{8,16},{12,20},{16,8},{20,12},{24,0},{28,4},{1,25},{... | collective-permute-start | bytes 368648 | tf_op jit(solution)/shard_map/ppermute | solution.py:743
  237.5 12.9 %collective-permute-start.52 = (bf16[48,1024]{1,0:T(8,128)(2,1)S(1)}, bf16[48,1024]{1,0:T(8,128)(2,1)S(1)}, u32[]{:S(2)}, u32[]{:S(2)}) collective-permute-start(bf16[48,1024]{1,0:T(8,128)(2,1)S(1)} %get-tuple-element.114), channel_id=1, source_target_pairs={{0,16},{4,20},{8,24},{12,28},{16,0},{20,4},{24,8},{28,12},{1,17},{... | collective-permute-start | bytes 294920 | tf_op jit(solution)/shard_map/ppermute | solution.py:743
  248.1 20.1 %collective-permute-start.56 = (bf16[2,4,48,1408]{3,2,1,0:T(8,128)(2,1)S(1)}, bf16[2,4,48,1408]{3,2,1,0:T(8,128)(2,1)S(1)}, u32[]{:S(2)}, u32[]{:S(2)}) collective-permute-start(bf16[2,4,48,1408]{3,2,1,0:T(8,128)(2,1)S(1)} %copy-done.26), channel_id=1, source_target_pairs={{0,2},{1,3},{2,0},{3,1},{4,6},{5,7},{6,4},{7,5},{8,10},{9,11},{10,... | collective-permute-start | bytes 3244040 | tf_op jit(solution)/shard_map/ppermute | solution.py:751
  249.6 16.8 %collective-permute-start.46 = (bf16[24,640]{1,0:T(8,128)(2,1)S(1)}, bf16[24,640]{1,0:T(8,128)(2,1)S(1)}, u32[]{:S(2)}, u32[]{:S(2)}) collective-permute-start(bf16[24,640]{1,0:T(8,128)(2,1)S(1)} %get-tuple-element.134), channel_id=1, source_target_pairs={{0,3},{1,2},{2,1},{3,0},{4,7},{5,6},{6,5},{7,4},{8,11},{9,10},{10,... | collective-permute-start | bytes 92168 | tf_op jit(solution)/shard_map/ppermute | solution.py:751
  250.4 17.5 %collective-permute-start.47 = (bf16[24,640]{1,0:T(8,128)(2,1)S(1)}, bf16[24,640]{1,0:T(8,128)(2,1)S(1)}, u32[]{:S(2)}, u32[]{:S(2)}) collective-permute-start(bf16[24,640]{1,0:T(8,128)(2,1)S(1)} %get-tuple-element.85), channel_id=1, source_target_pairs={{0,2},{1,3},{2,0},{3,1},{4,6},{5,7},{6,4},{7,5},{8,10},{9,11},{10,... | collective-permute-start | bytes 92168 | tf_op jit(solution)/shard_map/ppermute | solution.py:751
  252.5 15.4 %collective-permute-start.48 = (bf16[24,640]{1,0:T(8,128)(2,1)S(1)}, bf16[24,640]{1,0:T(8,128)(2,1)S(1)}, u32[]{:S(2)}, u32[]{:S(2)}) collective-permute-start(bf16[24,640]{1,0:T(8,128)(2,1)S(1)} %get-tuple-element.133), channel_id=1, source_target_pairs={{0,1},{1,0},{2,3},{3,2},{4,5},{5,4},{6,7},{7,6},{8,9},{9,8},{10,11... | collective-permute-start | bytes 92168 | tf_op jit(solution)/shard_map/ppermute | solution.py:751
  268.5 13.7 %collective-permute-start.57 = (bf16[4,48,1408]{2,1,0:T(8,128)(2,1)S(1)}, bf16[4,48,1408]{2,1,0:T(8,128)(2,1)S(1)}, u32[]{:S(2)}, u32[]{:S(2)}) collective-permute-start(bf16[4,48,1408]{2,1,0:T(8,128)(2,1)S(1)} %slice_bitcast_fusion), channel_id=1, source_target_pairs={{0,4},{4,0},{8,12},{12,8},{16,20},{20,16},{24,28},{28,24},{1,5},{5... | collective-permute-start | bytes 1622024 | tf_op jit(solution)/shard_map/ppermute | solution.py:747
  288.1 12.0 %collective-permute-start.59 = (bf16[48,1408]{1,0:T(8,128)(2,1)S(1)}, bf16[48,1408]{1,0:T(8,128)(2,1)S(1)}, u32[]{:S(2)}, u32[]{:S(2)}) collective-permute-start(bf16[48,1408]{1,0:T(8,128)(2,1)S(1)} %get-tuple-element.94), channel_id=1, source_target_pairs={{0,16},{4,20},{8,24},{12,28},{16,0},{20,4},{24,8},{28,12},{1,17},{... | collective-permute-start | bytes 405512 | tf_op jit(solution)/shard_map/ppermute | solution.py:743
  291.3 11.1 %collective-permute-start.41 = (bf16[256,768]{1,0:T(8,128)(2,1)S(1)}, bf16[256,768]{1,0:T(8,128)(2,1)S(1)}, u32[]{:S(2)}, u32[]{:S(2)}) collective-permute-start(bf16[256,768]{1,0:T(8,128)(2,1)S(1)} %get-tuple-element.88), channel_id=1, source_target_pairs={{0,2},{1,3},{2,0},{3,1},{4,6},{5,7},{6,4},{7,5},{8,10},{9,11},{10,... | collective-permute-start | bytes 1179656 | tf_op jit(solution)/shard_map/ppermute | solution.py:751
  (63 other events, 709.8 us)
